TPU v7x, 128 devices: a whole 4x4x4 slice. The times are simulated.
128 devices in a mesh: segment: 8 (over z, x_lo), coil: 16 (over y, x_hi, core).
Axes of the slice: x: 4 (x_hi: 2, x_lo: 2; x = x_hi * 2 + x_lo), y: 4, z: 4, core: 2. Of those that a mesh axis runs over, the one named last changes fastest.
Arguments:
- measured: float32 [16, 2, 320, 128], P('coil'), may hold values from -6 to 6
- coil_maps: float32 [16, 2, 320, 128], P('coil'), may hold values from -4 to 4
- line_mask: int32 [16, 320], replicated, may hold values 0 or 1
- first_filters: float32 [8, 64, 18], P('segment'), may hold values from -1.5 to 1.5
- second_filters: float32 [8, 18, 64], P('segment'), may hold values from -0.075 to 0.075
- step_sizes: float32 [8], P('segment'), may hold values from 0.2 to 1
- final_cotangent: float32 [16, 2, 320, 128], P('coil'), may hold values from -6 to 6
Outputs:
- kspace_grads: float32 [8, 16, 2, 320, 128], P('segment', 'coil')
- first_grads: float32 [8, 64, 18], P('segment')
- second_grads: float32 [8, 18, 64], P('segment')
- step_grads: float32 [8], P('segment')
All inputs are finite; a program needn't handle non-finite values.
Results may differ from a plain program's by a relative error of at most 0.0003.
Values sent between devices are 32-bit elements; how exact they have to be, the bound alone decides.
A program may use at most 320 MiB of HBM per device.

v0:
```python
from functools import partial

import jax
import jax.numpy as jnp
from jax import lax
from jax.sharding import PartitionSpec as P

PRECISE = lax.Precision.HIGHEST
tap_offsets = ((-1, -1), (-1, 0), (-1, 1), (0, -1), (0, 0), (0, 1), (1, -1), (1, 0), (1, 1))


def from_behind(block, axis, distance):
    devices = range(lax.axis_size(axis))
    route = [(i - distance, i) for i in devices if i - distance in devices]
    return lax.ppermute(block, axis, route)


def tables(line_count):
    positions = jnp.arange(line_count, dtype=jnp.int32)
    products = positions[:, None] * positions[None, :] % line_count
    angles = 2.0 * jnp.pi / line_count * products.astype(jnp.float32)
    factor = 1.0 / jnp.sqrt(jnp.float32(line_count))
    return (jnp.cos(angles) * factor, jnp.sin(angles) * factor)


def multiply_lines(table, operand):
    return jnp.einsum("uh,chx->cux", table, operand, precision=PRECISE)


def multiply_slices(table, operand, slice_width):
    count, lines, columns = operand.shape
    shaped = operand.reshape(count, lines, columns // slice_width, slice_width)
    result = jnp.einsum("us,chsw->chuw", table, shaped, precision=PRECISE)
    return result.reshape(count, lines, table.shape[0] * slice_width)


def rotate(cosine_table, sine_table, real_part, imag_part, applier, inverse):
    if inverse:
        out_real = applier(cosine_table, real_part) - applier(sine_table, imag_part)
        out_imag = applier(cosine_table, imag_part) + applier(sine_table, real_part)
    else:
        out_real = applier(cosine_table, real_part) + applier(sine_table, imag_part)
        out_imag = applier(cosine_table, imag_part) - applier(sine_table, real_part)
    return (out_real, out_imag)


def transform(kspace, line_tables, slice_tables, slice_width):
    real_part, imag_part = rotate(
        line_tables[0], line_tables[1], kspace[:, 0], kspace[:, 1], multiply_lines, True
    )
    real_part, imag_part = rotate(
        slice_tables[0],
        slice_tables[1],
        real_part,
        imag_part,
        partial(multiply_slices, slice_width=slice_width),
        True,
    )
    return jnp.stack([real_part, imag_part], axis=1)


def conj_product(coil_maps, kspace):
    real_part = coil_maps[:, 0] * kspace[:, 0] + coil_maps[:, 1] * kspace[:, 1]
    imag_part = coil_maps[:, 0] * kspace[:, 1] - coil_maps[:, 1] * kspace[:, 0]
    return jnp.stack([jnp.sum(real_part, axis=0), jnp.sum(imag_part, axis=0)])


def spread(coil_maps, picture):
    real_part = coil_maps[:, 0] * picture[0] - coil_maps[:, 1] * picture[1]
    imag_part = coil_maps[:, 0] * picture[1] + coil_maps[:, 1] * picture[0]
    return jnp.stack([real_part, imag_part], axis=1)


def moved(values, row_shift, col_shift, slice_width):
    total = values.shape[-1]
    margin = slice_width + 1
    padded = jnp.pad(values, ((0, 0), (margin, margin)))
    offset = margin + row_shift * slice_width + col_shift
    shifted = lax.slice_in_dim(padded, offset, offset + total, axis=1)
    column = jnp.arange(total, dtype=jnp.int32) % slice_width
    inside = (column + col_shift >= 0) & (column + col_shift < slice_width)
    return jnp.where(inside[None, :], shifted, jnp.zeros_like(shifted))


def network(picture, filters_in, filters_out, slice_width):
    stacked = jnp.stack([moved(picture, pair[0], pair[1], slice_width) for pair in tap_offsets])
    stacked = jnp.transpose(stacked, (1, 0, 2)).reshape(18, picture.shape[-1])
    hidden = jax.nn.silu(jnp.dot(filters_in, stacked, precision=PRECISE))
    response = jnp.dot(filters_out, hidden, precision=PRECISE).reshape(2, 9, picture.shape[-1])
    result = jnp.zeros_like(picture)
    for number, pair in enumerate(tap_offsets):
        result = result + moved(response[:, number], pair[0], pair[1], slice_width)
    return result


def refine(picture, filters_in, filters_out, slice_width):
    line_count = picture.shape[1]
    columns = picture.shape[2]
    count = columns // slice_width
    per_slice = picture.reshape(2, line_count, count, slice_width).transpose(2, 0, 1, 3)
    per_slice = per_slice.reshape(count, 2, line_count * slice_width)
    outcome = jax.vmap(lambda single: network(single, filters_in, filters_out, slice_width))(
        per_slice
    )
    outcome = outcome.reshape(count, 2, line_count, slice_width).transpose(1, 2, 0, 3)
    return outcome.reshape(2, line_count, columns)


def shards(
    measured, coil_maps, line_mask, first_filters, second_filters, step_sizes, final_cotangent
):
    line_count = measured.shape[2]
    columns = measured.shape[3]
    slice_count = line_mask.shape[0]
    slice_width = columns // slice_count
    line_tables = tables(line_count)
    slice_tables = tables(slice_count)
    sampled = jnp.repeat(line_mask.T.astype(jnp.float32), slice_width, axis=1)
    sampled_data = measured * sampled
    segment_index = lax.axis_index("segment")
    sections = lax.axis_size("segment")
    step_size = step_sizes[0]
    weight_in = first_filters[0]
    weight_out = second_filters[0]

    def collect(kspace):
        partial_image = conj_product(
            coil_maps, transform(kspace, line_tables, slice_tables, slice_width)
        )
        return lax.psum_scatter(partial_image, "coil", scatter_dimension=2, tiled=True)

    def return_field(refined):
        field = spread(coil_maps, lax.all_gather(refined, "coil", axis=2, tiled=True))
        real_part, imag_part = rotate(
            line_tables[0], line_tables[1], field[:, 0], field[:, 1], multiply_lines, False
        )
        part_cosine = slice_tables[0]
        part_sine = slice_tables[1]
        real_part, imag_part = rotate(
            part_cosine,
            part_sine,
            real_part,
            imag_part,
            partial(multiply_slices, slice_width=slice_width),
            False,
        )
        return jnp.stack([real_part, imag_part], axis=1)

    current = sampled_data
    saved_k = sampled_data
    saved_y = None
    for turn_index in range(sections):
        combined = collect(current)
        active = segment_index == turn_index
        saved_k = jnp.where(active, current, saved_k)
        if saved_y is None:
            saved_y = jnp.where(active, combined, jnp.zeros_like(combined))
        else:
            saved_y = jnp.where(active, combined, saved_y)
        if turn_index + 1 < sections:
            refined = refine(combined, weight_in, weight_out, slice_width)
            updated = (
                current - step_size * sampled * (current - sampled_data) + return_field(refined)
            )
            current = from_behind(updated, "segment", 1)
    final_segment = sections - 1
    flowing = jnp.where(
        segment_index == final_segment, final_cotangent, jnp.zeros_like(final_cotangent)
    )
    grad_k = jnp.zeros_like(sampled_data)
    grad_in = jnp.zeros_like(weight_in)
    grad_out = jnp.zeros_like(weight_out)
    grad_step = jnp.zeros((), jnp.float32)

    def local_refine(picture, filters_in, filters_out):
        return refine(picture, filters_in, filters_out, slice_width)

    for turn_index in range(sections):
        active = segment_index == final_segment - turn_index
        back_image = collect(flowing)
        _, pullback = jax.vjp(local_refine, saved_y, weight_in, weight_out)
        d_image, d_first, d_second = pullback(back_image)
        inward = flowing - step_size * sampled * flowing + return_field(d_image)
        grad_k = jnp.where(active, inward, grad_k)
        grad_in = grad_in + jnp.where(active, d_first, jnp.zeros_like(d_first))
        grad_out = grad_out + jnp.where(active, d_second, jnp.zeros_like(d_second))
        step_term = -jnp.sum(sampled * (saved_k - sampled_data) * flowing)
        grad_step = grad_step + jnp.where(active, step_term, jnp.zeros_like(step_term))
        if turn_index + 1 < sections:
            flowing = from_behind(inward, "segment", -1)
    grad_in, grad_out, grad_step = lax.psum((grad_in, grad_out, grad_step), "coil")
    return (grad_k[None], grad_in[None], grad_out[None], grad_step.reshape(1))


def solution(mesh):
    in_specs = (
        P("coil", None, None, None),
        P("coil", None, None, None),
        P(),
        P("segment", None, None),
        P("segment", None, None),
        P("segment"),
        P("coil", None, None, None),
    )
    out_specs = (
        P("segment", "coil", None, None, None),
        P("segment", None, None),
        P("segment", None, None),
        P("segment"),
    )
    return jax.shard_map(shards, mesh=mesh, in_specs=in_specs, out_specs=out_specs, check_vma=False)
```

profile of v0, /device:TPU:1, one launch (start us, length us, event | category | flops | bytes accessed | tf_op | source)
XLA Modules:
  0.0 2194.0 jit_solution(9464638714813180581)
XLA Ops:
  35.8 63.5 %reduce-scatter.19.cloned.1.call-done = f32[2,320,8]{1,2,0:T(8,128)} async-done(((f32[2,320,128]{1,2,0:T(8,128)}), f32[2,320,8]{1,2,0:T(8,128)}) %reduce-scatter.19.cloned.1.call-update) | async-done | bytes 20496 | tf_op jit(solution)/shard_map/reduce_scatter | solution.py:130
  100.6 65.4 %reduce-scatter.17.cloned.1.call-done = f32[2,320,8]{1,2,0:T(8,128)} async-done(((f32[2,320,128]{1,2,0:T(8,128)}), f32[2,320,8]{1,2,0:T(8,128)}) %reduce-scatter.17.cloned.1.call-update) | async-done | bytes 20496 | tf_op jit(solution)/shard_map/reduce_scatter | solution.py:130
  170.9 25.5 %all_gather.45 = f32[2,320,128]{1,2,0:T(8,128)S(1)} all-gather(f32[2,320,8]{1,2,0:T(8,128)S(1)} %copy.664), channel_id=1, replica_groups=mesh['segment'=8,'coil'=16] {'coil'}, dimensions={2}, use_global_device_ids=true | all-gather | bytes 348160 | tf_op jit(solution)/shard_map/all_gather | solution.py:133
  234.4 61.0 %reduce-scatter.21.cloned.1.call-done = f32[2,320,8]{1,2,0:T(8,128)} async-done(((f32[2,320,128]{1,2,0:T(8,128)}), f32[2,320,8]{1,2,0:T(8,128)}) %reduce-scatter.21.cloned.1.call-update) | async-done | bytes 20496 | tf_op jit(solution)/shard_map/reduce_scatter | solution.py:130
  299.9 25.5 %all_gather.46 = f32[2,320,128]{1,2,0:T(8,128)S(1)} all-gather(f32[2,320,8]{1,2,0:T(8,128)S(1)} %copy.693), channel_id=1, replica_groups=mesh['segment'=8,'coil'=16] {'coil'}, dimensions={2}, use_global_device_ids=true | all-gather | bytes 348160 | tf_op jit(solution)/shard_map/all_gather | solution.py:133
  363.7 60.8 %reduce-scatter.23.cloned.1.call-done = f32[2,320,8]{1,2,0:T(8,128)} async-done(((f32[2,320,128]{1,2,0:T(8,128)}), f32[2,320,8]{1,2,0:T(8,128)}) %reduce-scatter.23.cloned.1.call-update) | async-done | bytes 20496 | tf_op jit(solution)/shard_map/reduce_scatter | solution.py:130
  429.0 25.5 %all_gather.47 = f32[2,320,128]{1,2,0:T(8,128)S(1)} all-gather(f32[2,320,8]{1,2,0:T(8,128)S(1)} %copy.722), channel_id=1, replica_groups=mesh['segment'=8,'coil'=16] {'coil'}, dimensions={2}, use_global_device_ids=true | all-gather | bytes 348160 | tf_op jit(solution)/shard_map/all_gather | solution.py:133
  492.6 61.0 %reduce-scatter.25.cloned.1.call-done = f32[2,320,8]{1,2,0:T(8,128)} async-done(((f32[2,320,128]{1,2,0:T(8,128)}), f32[2,320,8]{1,2,0:T(8,128)}) %reduce-scatter.25.cloned.1.call-update) | async-done | bytes 20496 | tf_op jit(solution)/shard_map/reduce_scatter | solution.py:130
  558.0 25.5 %all_gather.48 = f32[2,320,128]{1,2,0:T(8,128)S(1)} all-gather(f32[2,320,8]{1,2,0:T(8,128)S(1)} %copy.751), channel_id=1, replica_groups=mesh['segment'=8,'coil'=16] {'coil'}, dimensions={2}, use_global_device_ids=true | all-gather | bytes 348160 | tf_op jit(solution)/shard_map/all_gather | solution.py:133
  621.6 61.1 %reduce-scatter.27.cloned.1.call-done = f32[2,320,8]{1,2,0:T(8,128)} async-done(((f32[2,320,128]{1,2,0:T(8,128)}), f32[2,320,8]{1,2,0:T(8,128)}) %reduce-scatter.27.cloned.1.call-update) | async-done | bytes 20496 | tf_op jit(solution)/shard_map/reduce_scatter | solution.py:130
  687.1 25.5 %all_gather.49 = f32[2,320,128]{1,2,0:T(8,128)S(1)} all-gather(f32[2,320,8]{1,2,0:T(8,128)S(1)} %copy.780), channel_id=1, replica_groups=mesh['segment'=8,'coil'=16] {'coil'}, dimensions={2}, use_global_device_ids=true | all-gather | bytes 348160 | tf_op jit(solution)/shard_map/all_gather | solution.py:133
  750.9 60.8 %reduce-scatter.29.cloned.1.call-done = f32[2,320,8]{1,2,0:T(8,128)} async-done(((f32[2,320,128]{1,2,0:T(8,128)}), f32[2,320,8]{1,2,0:T(8,128)}) %reduce-scatter.29.cloned.1.call-update) | async-done | bytes 20496 | tf_op jit(solution)/shard_map/reduce_scatter | solution.py:130
  816.2 25.5 %all_gather.50 = f32[2,320,128]{1,2,0:T(8,128)S(1)} all-gather(f32[2,320,8]{1,2,0:T(8,128)S(1)} %copy.809), channel_id=1, replica_groups=mesh['segment'=8,'coil'=16] {'coil'}, dimensions={2}, use_global_device_ids=true | all-gather | bytes 348160 | tf_op jit(solution)/shard_map/all_gather | solution.py:133
  880.0 60.9 %reduce-scatter.31.cloned.1.call-done = f32[2,320,8]{1,2,0:T(8,128)} async-done(((f32[2,320,128]{1,2,0:T(8,128)}), f32[2,320,8]{1,2,0:T(8,128)}) %reduce-scatter.31.cloned.1.call-update) | async-done | bytes 20496 | tf_op jit(solution)/shard_map/reduce_scatter | solution.py:130
  945.3 25.5 %all_gather.51 = f32[2,320,128]{1,2,0:T(8,128)S(1)} all-gather(f32[2,320,8]{1,2,0:T(8,128)S(1)} %copy.838), channel_id=1, replica_groups=mesh['segment'=8,'coil'=16] {'coil'}, dimensions={2}, use_global_device_ids=true | all-gather | bytes 348160 | tf_op jit(solution)/shard_map/all_gather | solution.py:133
  1009.3 60.9 %reduce-scatter.33.cloned.1.call-done = f32[2,320,8]{1,2,0:T(8,128)} async-done(((f32[2,320,128]{1,2,0:T(8,128)}), f32[2,320,8]{1,2,0:T(8,128)}) %reduce-scatter.33.cloned.1.call-update) | async-done | bytes 20496 | tf_op jit(solution)/shard_map/reduce_scatter | solution.py:130
  1075.6 25.5 %all_gather.52 = f32[2,320,128]{1,2,0:T(8,128)S(1)} all-gather(f32[2,320,8]{1,2,0:T(8,128)S(1)} %copy.859), channel_id=1, replica_groups=mesh['segment'=8,'coil'=16] {'coil'}, dimensions={2}, use_global_device_ids=true | all-gather | bytes 348160 | tf_op jit(solution)/shard_map/all_gather | solution.py:133
  1141.3 59.9 %reduce-scatter.35.cloned.1.call-done = f32[2,320,8]{1,2,0:T(8,128)} async-done(((f32[2,320,128]{1,2,0:T(8,128)}), f32[2,320,8]{1,2,0:T(8,128)}) %reduce-scatter.35.cloned.1.call-update) | async-done | bytes 20496 | tf_op jit(solution)/shard_map/reduce_scatter | solution.py:130
  1206.3 25.5 %all_gather.53 = f32[2,320,128]{1,2,0:T(8,128)S(1)} all-gather(f32[2,320,8]{1,2,0:T(8,128)S(1)} %copy.880), channel_id=1, replica_groups=mesh['segment'=8,'coil'=16] {'coil'}, dimensions={2}, use_global_device_ids=true | all-gather | bytes 348160 | tf_op jit(solution)/shard_map/all_gather | solution.py:133
  1271.7 60.1 %reduce-scatter.37.cloned.1.call-done = f32[2,320,8]{1,2,0:T(8,128)} async-done(((f32[2,320,128]{1,2,0:T(8,128)}), f32[2,320,8]{1,2,0:T(8,128)}) %reduce-scatter.37.cloned.1.call-update) | async-done | bytes 20496 | tf_op jit(solution)/shard_map/reduce_scatter | solution.py:130
  1338.0 25.5 %all_gather.54 = f32[2,320,128]{1,2,0:T(8,128)S(1)} all-gather(f32[2,320,8]{1,2,0:T(8,128)S(1)} %copy.901), channel_id=1, replica_groups=mesh['segment'=8,'coil'=16] {'coil'}, dimensions={2}, use_global_device_ids=true | all-gather | bytes 348160 | tf_op jit(solution)/shard_map/all_gather | solution.py:133
  1405.2 60.2 %reduce-scatter.39.cloned.1.call-done = f32[2,320,8]{1,2,0:T(8,128)} async-done(((f32[2,320,128]{1,2,0:T(8,128)}), f32[2,320,8]{1,2,0:T(8,128)}) %reduce-scatter.39.cloned.1.call-update) | async-done | bytes 20496 | tf_op jit(solution)/shard_map/reduce_scatter | solution.py:130
  1472.3 25.5 %all_gather.55 = f32[2,320,128]{1,2,0:T(8,128)S(1)} all-gather(f32[2,320,8]{1,2,0:T(8,128)S(1)} %copy.922), channel_id=1, replica_groups=mesh['segment'=8,'coil'=16] {'coil'}, dimensions={2}, use_global_device_ids=true | all-gather | bytes 348160 | tf_op jit(solution)/shard_map/all_gather | solution.py:133
  1548.2 57.4 %reduce-scatter.41.cloned.1.call-done = f32[2,320,8]{1,2,0:T(8,128)} async-done(((f32[2,320,128]{1,2,0:T(8,128)}), f32[2,320,8]{1,2,0:T(8,128)}) %reduce-scatter.41.cloned.1.call-update) | async-done | bytes 20496 | tf_op jit(solution)/shard_map/reduce_scatter | solution.py:130
  1621.8 25.5 %all_gather.56 = f32[2,320,128]{1,2,0:T(8,128)S(1)} all-gather(f32[2,320,8]{1,2,0:T(8,128)S(1)} %copy.943), channel_id=1, replica_groups=mesh['segment'=8,'coil'=16] {'coil'}, dimensions={2}, use_global_device_ids=true | all-gather | bytes 348160 | tf_op jit(solution)/shard_map/all_gather | solution.py:133
  1702.4 57.6 %reduce-scatter.43.cloned.1.call-done = f32[2,320,8]{1,2,0:T(8,128)} async-done(((f32[2,320,128]{1,2,0:T(8,128)}), f32[2,320,8]{1,2,0:T(8,128)}) %reduce-scatter.43.cloned.1.call-update) | async-done | bytes 20496 | tf_op jit(solution)/shard_map/reduce_scatter | solution.py:130
  1776.2 25.5 %all_gather.57 = f32[2,320,128]{1,2,0:T(8,128)S(1)} all-gather(f32[2,320,8]{1,2,0:T(8,128)S(1)} %copy.964), channel_id=1, replica_groups=mesh['segment'=8,'coil'=16] {'coil'}, dimensions={2}, use_global_device_ids=true | all-gather | bytes 348160 | tf_op jit(solution)/shard_map/all_gather | solution.py:133
  1856.9 57.7 %reduce-scatter.45.cloned.1.call-done = f32[2,320,8]{1,2,0:T(8,128)} async-done(((f32[2,320,128]{1,2,0:T(8,128)}), f32[2,320,8]{1,2,0:T(8,128)}) %reduce-scatter.45.cloned.1.call-update) | async-done | bytes 20496 | tf_op jit(solution)/shard_map/reduce_scatter | solution.py:130
  1930.8 25.5 %all_gather.58 = f32[2,320,128]{1,2,0:T(8,128)S(1)} all-gather(f32[2,320,8]{1,2,0:T(8,128)S(1)} %copy.985), channel_id=1, replica_groups=mesh['segment'=8,'coil'=16] {'coil'}, dimensions={2}, use_global_device_ids=true | all-gather | bytes 348160 | tf_op jit(solution)/shard_map/all_gather | solution.py:133
  2018.0 51.1 %reduce-scatter.47.cloned.1.call-done = f32[2,320,8]{1,2,0:T(8,128)} async-done(((f32[2,320,128]{1,2,0:T(8,128)}), f32[2,320,8]{1,2,0:T(8,128)}) %reduce-scatter.47.cloned.1.call-update) | async-done | bytes 20496 | tf_op jit(solution)/shard_map/reduce_scatter | solution.py:130
  2076.0 62.6 %all-reduce.264 = (f32[1,64,18]{1,2,0:T(8,128)S(1)}, f32[1,18,64]{2,1,0:T(8,128)S(1)}, f32[1]{0:T(128)}) all-reduce(f32[1,64,18]{1,2,0:T(8,128)S(1)} %fusion.133, f32[1,18,64]{2,1,0:T(8,128)S(1)} %fusion.125, f32[1]{0:T(128)} %bitcast.790), channel_id=1, replica_groups=mesh['segment'=8,'coil'=16] {'coil'}, use_global_device_ids=true, to_apply=%region_16.17 | all-reduce | flops 2305 | bytes 18440 | tf_op jit(solution)/shard_map/psum | solution.py:191
  2140.5 26.8 %all_gather.59 = f32[2,320,128]{1,2,0:T(8,128)S(1)} all-gather(f32[2,320,8]{1,2,0:T(8,128)S(1)} %copy.1006), channel_id=1, replica_groups=mesh['segment'=8,'coil'=16] {'coil'}, dimensions={2}, use_global_device_ids=true | all-gather | bytes 348160 | tf_op jit(solution)/shard_map/all_gather | solution.py:133
  (1056 shorter events, 762.8 us)
Async XLA Ops:
  7.2 92.1 %reduce-scatter.19.cloned.1.call-start = ((), (), s32[]{:S(2)}) async-start(), calls=%async_computation.17 | async-start | bytes 417792 | tf_op jit(solution)/shard_map/reduce_scatter | solution.py:130
  34.0 132.0 %reduce-scatter.17.cloned.1.call-start = ((), (), s32[]{:S(2)}) async-start(), calls=%async_computation.16 | async-start | bytes 417792 | tf_op jit(solution)/shard_map/reduce_scatter | solution.py:130
  34.8 260.7 %reduce-scatter.21.cloned.1.call-start = ((), (), s32[]{:S(2)}) async-start(), calls=%async_computation.18 | async-start | bytes 417792 | tf_op jit(solution)/shard_map/reduce_scatter | solution.py:130
  210.5 11.3 collective-permute-start
  234.2 190.3 %reduce-scatter.23.cloned.1.call-start = ((), (), s32[]{:S(2)}) async-start(), calls=%async_computation.19 | async-start | bytes 417792 | tf_op jit(solution)/shard_map/reduce_scatter | solution.py:130
  339.6 11.2 collective-permute-start.1
  363.3 190.3 %reduce-scatter.25.cloned.1.call-start = ((), (), s32[]{:S(2)}) async-start(), calls=%async_computation.20 | async-start | bytes 417792 | tf_op jit(solution)/shard_map/reduce_scatter | solution.py:130
  468.6 11.2 collective-permute-start.2
  492.3 190.3 %reduce-scatter.27.cloned.1.call-start = ((), (), s32[]{:S(2)}) async-start(), calls=%async_computation.21 | async-start | bytes 417792 | tf_op jit(solution)/shard_map/reduce_scatter | solution.py:130
  597.7 11.2 collective-permute-start.3
  621.4 190.4 %reduce-scatter.29.cloned.1.call-start = ((), (), s32[]{:S(2)}) async-start(), calls=%async_computation.22 | async-start | bytes 417792 | tf_op jit(solution)/shard_map/reduce_scatter | solution.py:130
  726.8 11.2 collective-permute-start.4
  750.5 190.4 %reduce-scatter.31.cloned.1.call-start = ((), (), s32[]{:S(2)}) async-start(), calls=%async_computation.23 | async-start | bytes 417792 | tf_op jit(solution)/shard_map/reduce_scatter | solution.py:130
  855.9 11.2 collective-permute-start.5
  867.1 117.8 %copy-start.66 = (f32[1,2,320,128]{2,3,1,0:T(8,128)}, f32[1,2,320,128]{2,3,1,0:T(8,128)S(1)}, u32[]{:S(2)}) copy-start(f32[1,2,320,128]{2,3,1,0:T(8,128)S(1)} %collective-permute-done.5) | copy-start | bytes 983044
  879.6 190.6 %reduce-scatter.33.cloned.1.call-start = ((), (), s32[]{:S(2)}) async-start(), calls=%async_computation.24 | async-start | bytes 417792 | tf_op jit(solution)/shard_map/reduce_scatter | solution.py:130
  985.0 11.2 collective-permute-start.6
  1008.7 192.4 %reduce-scatter.35.cloned.1.call-start = ((), (), s32[]{:S(2)}) async-start(), calls=%async_computation.25 | async-start | bytes 417792 | tf_op jit(solution)/shard_map/reduce_scatter | solution.py:130
  1072.4 130.6 %copy-start.67 = (f32[2560,64]{0,1:T(8,128)}, f32[2560,64]{0,1:T(8,128)S(1)}, u32[]{:S(2)}) copy-start(f32[2560,64]{0,1:T(8,128)S(1)} %fusion.929) | copy-start | bytes 1966084
  1115.9 12.5 collective-permute-start.7
  1140.8 191.0 %reduce-scatter.37.cloned.1.call-start = ((), (), s32[]{:S(2)}) async-start(), calls=%async_computation.26 | async-start | bytes 417792 | tf_op jit(solution)/shard_map/reduce_scatter | solution.py:130
  1246.5 12.4 collective-permute-start.8
  1271.4 194.0 %reduce-scatter.39.cloned.1.call-start = ((), (), s32[]{:S(2)}) async-start(), calls=%async_computation.27 | async-start | bytes 417792 | tf_op jit(solution)/shard_map/reduce_scatter | solution.py:130
  1378.3 12.4 collective-permute-start.9
  1405.0 200.6 %reduce-scatter.41.cloned.1.call-start = ((), (), s32[]{:S(2)}) async-start(), calls=%async_computation.28 | async-start | bytes 417792 | tf_op jit(solution)/shard_map/reduce_scatter | solution.py:130
  1513.5 12.6 collective-permute-start.10
  1545.2 214.8 %reduce-scatter.43.cloned.1.call-start = ((), (), s32[]{:S(2)}) async-start(), calls=%async_computation.29 | async-start | bytes 417792 | tf_op jit(solution)/shard_map/reduce_scatter | solution.py:130
  1666.9 12.6 collective-permute-start.11
  1699.6 215.0 %reduce-scatter.45.cloned.1.call-start = ((), (), s32[]{:S(2)}) async-start(), calls=%async_computation.30 | async-start | bytes 417792 | tf_op jit(solution)/shard_map/reduce_scatter | solution.py:130
  1821.6 12.6 collective-permute-start.12
  1854.1 215.0 %reduce-scatter.47.cloned.1.call-start = ((), (), s32[]{:S(2)}) async-start(), calls=%async_computation.31 | async-start | bytes 417792 | tf_op jit(solution)/shard_map/reduce_scatter | solution.py:130
  1976.2 12.6 collective-permute-start.13
  (96 other events, 1203.9 us)
Sparse Core Ops, SparseCore 0:
  34.1 65.1 reduce-scatter.18
  103.1 62.8 reduce-scatter.16
  234.3 61.0 reduce-scatter.20
  363.4 61.0 reduce-scatter.22
  492.4 61.0 reduce-scatter.24
  621.5 61.1 reduce-scatter.26
  750.6 61.0 reduce-scatter.28
  879.7 61.1 reduce-scatter.30
  1008.8 61.2 reduce-scatter.32
  1140.9 60.1 reduce-scatter.34
  1271.5 60.2 reduce-scatter.36
  1405.1 60.2 reduce-scatter.38
  1545.3 60.2 reduce-scatter.40
  1699.7 60.2 reduce-scatter.42
  1854.3 60.2 reduce-scatter.44
  2008.9 60.1 reduce-scatter.46
where the time goes:
time: 2210 us; the launch traced here: 2190 us
  waiting for transfers between devices  1090 us (49%)
  matrix products  446 us (20%)
  blocking collectives  446 us (20%)
  local copies, waits for them, and re-layouts  117 us (5%)
  starting transfers between devices  37.8 us (2%)
  other arithmetic  34.2 us (2%)
  between operations  25.8 us (1%)
    reduce_scatter x16, waiting for transfers between devices, collect(): lax.psum_scatter(partial_image, 'coil', scatter_dimension=2, tiled=True)  959 us
    all_gather x15, blocking collectives, return_field(): lax.all_gather(refined, 'coil', axis=2, tiled=True)  384 us
    dot_general x124, matrix products, multiply_lines(): return jnp.einsum('uh,chx->cux', table, operand, precision=PRECISE)  348 us
    ppermute x14, waiting for transfers between devices, from_behind(): return lax.ppermute(block, axis, route)  127 us
    psum x1, blocking collectives, shards(): lax.psum((grad_in, grad_out, grad_step), 'coil')  62.6 us
    dot_general x124, matrix products, multiply_slices(): result = jnp.einsum('us,chsw->chuw', table, shaped, precision=PRECISE)  52.4 us
  transfers between devices with their start and end apart: 30, of which 30 were waited for; matrix products, arithmetic and copies ran while one was open for 1% of the time, Pallas kernels for 0%

commit v1 on v0

v1 whole, which is shorter than its diff:
```python
import functools

import jax
import jax.numpy as jnp
import ml_dtypes
import numpy as np
from jax import lax
from jax.experimental import pallas as pl
from jax.experimental.pallas import tpu as pltpu
from jax.sharding import PartitionSpec as P

F32 = jnp.float32
BF16 = jnp.bfloat16
LINES = 320
QUARTER = 80
LANES = 128
WIDTH = 8
SLICES = 16
COILS = 16
CASC = 8
STEPS = 2 * CASC
HIDDEN = 64
MESH = pl.DeviceIdType.MESH


def stacked(table):
    high = table.astype(ml_dtypes.bfloat16)
    low = (table - high.astype(np.float64)).astype(ml_dtypes.bfloat16)
    return np.concatenate([high, high, low], axis=-2)


@functools.lru_cache(maxsize=None)
def constants():
    forward = np.zeros((4, 256, 256))
    inverse = np.zeros((4, 256, 256))
    v = np.arange(QUARTER)[:, None]
    b = np.arange(QUARTER)[None, :]
    re, im = slice(0, QUARTER), slice(LANES, LANES + QUARTER)
    for m in range(4):
        angle = 2 * np.pi * (((4 * v + m) * b) % LINES) / LINES
        cosine = np.cos(angle) / np.sqrt(LINES)
        sine = np.sin(angle) / np.sqrt(LINES)
        forward[m, re, re] = cosine.T
        forward[m, re, im] = -sine.T
        forward[m, im, re] = sine.T
        forward[m, im, im] = cosine.T
        inverse[m, re, re] = cosine
        inverse[m, re, im] = sine
        inverse[m, im, re] = -sine
        inverse[m, im, im] = cosine
    tf = stacked(forward)
    ti = stacked(inverse)
    tft = np.ascontiguousarray(np.swapaxes(tf, 1, 2))

    perm = np.zeros((LANES, LANES), np.float32)
    dz = np.zeros((256, 256))
    for w in range(WIDTH):
        for s in range(SLICES):
            perm[w * SLICES + s, s * WIDTH + w] = 1
            for kz in range(SLICES):
                angle = 2 * np.pi * (s * kz % SLICES) / SLICES
                row, lane = w * SLICES + s, kz * WIDTH + w
                dz[row, lane] = np.cos(angle) / 4
                dz[row, LANES + lane] = -np.sin(angle) / 4
                dz[LANES + row, lane] = np.sin(angle) / 4
                dz[LANES + row, LANES + lane] = np.cos(angle) / 4
    dz = stacked(dz)

    rep = np.zeros((SLICES, LANES), np.float32)
    cz = np.zeros((WIDTH, 32, LANES), np.float32)
    gc = np.zeros((SLICES, 32, LANES), np.float32)
    for kz in range(SLICES):
        rep[kz, kz * WIDTH : (kz + 1) * WIDTH] = 1
        for s in range(SLICES):
            angle = 2 * np.pi * (s * kz % SLICES) / SLICES
            for w in range(WIDTH):
                cz[w, s, kz * WIDTH + w] = np.cos(angle) / 4
                cz[w, 16 + s, kz * WIDTH + w] = np.sin(angle) / 4
            for other in range(SLICES):
                angle = 2 * np.pi * ((s - other) * kz % SLICES) / SLICES
                gc[s, other, kz * WIDTH] = np.cos(angle) / 16
                gc[s, 16 + other, kz * WIDTH] = np.sin(angle) / 16

    expand = np.zeros((2, LANES, 4 * 256), np.float32)
    choose = np.zeros((2, 3 * 64, LANES), np.float32)
    fold = np.zeros((2, 24, LANES), np.float32)
    amask = np.zeros((64, 256), np.float32)
    gmask = np.zeros((256, LANES), np.float32)
    for ch in range(2):
        for dh in range(3):
            for dw in range(3):
                taps = (ch * 9 + dh * 3 + dw, ch * 9 + (2 - dh) * 3 + (2 - dw))
                for way in range(2):
                    for a in range(4):
                        lane = dw * 24 + dh * 8 + a * 2 + ch
                        expand[way, taps[way], a * 256 + lane] = 1
                        expand[way, taps[way], a * 256 + 72 + lane] = 1
                        expand[way, 24 + taps[way], a * 256 + 144 + lane] = 1
                        fold[way, taps[way], lane] = 1
                        for hl in range(2):
                            row = hl * 32 + dh * 8 + a * 2 + ch
                            choose[way, dw * 64 + row, hl * 24 + taps[way]] = 1
                            amask[row, a * 64 : (a + 1) * 64] = 1
                        gmask[a * 64 : (a + 1) * 64, lane] = 1
    bf = ml_dtypes.bfloat16
    return (
        tf, ti, tft, dz, perm, rep, cz, gc,
        expand.astype(bf), choose.astype(bf), fold, amask, gmask,
    )


def exact_nt(left, right):
    return lax.dot_general(
        left, right, (((1,), (1,)), ((), ())),
        precision=lax.Precision.HIGHEST, preferred_element_type=F32,
    )


def product(left, right):
    return jnp.dot(left, right, preferred_element_type=F32)


def product_nt(left, right):
    return lax.dot_general(left, right, (((1,), (1,)), ((), ())), preferred_element_type=F32)


def parts(values):
    high = values.astype(BF16)
    low = (values - high.astype(F32)).astype(BF16)
    return high, low


def triple(re, im):
    re_high, re_low = parts(re)
    im_high, im_low = parts(im)
    return jnp.concatenate([re_high, im_high, re_low, im_low, re_high, im_high], axis=1)


def shifted(tile):
    lane = lax.broadcasted_iota(jnp.int32, (8, LANES), 1)
    row = lax.broadcasted_iota(jnp.int32, (8, LANES), 0)
    zero = jnp.zeros_like(tile)
    last = QUARTER - 1
    next_first = pltpu.roll(pltpu.roll(tile, last, 1), 6, 0)
    after = jnp.where(
        lane < last,
        pltpu.roll(tile, LANES - 1, 1),
        jnp.where((lane == last) & (row < 6), next_first, zero),
    )
    previous_last = pltpu.roll(pltpu.roll(tile, LANES - last, 1), 2, 0)
    before = jnp.where(
        (lane >= 1) & (lane < QUARTER),
        pltpu.roll(tile, 1, 1),
        jnp.where((lane == 0) & (row >= 2), previous_last, zero),
    )
    return before, after


def quarters_to_residues(p):
    t0 = [p[0][k] + p[2][k] for k in range(2)]
    t1 = [p[0][k] - p[2][k] for k in range(2)]
    t2 = [p[1][k] + p[3][k] for k in range(2)]
    t3 = [p[1][k] - p[3][k] for k in range(2)]
    return (
        (t0[0] + t2[0], t0[1] + t2[1]),
        (t1[0] + t3[1], t1[1] - t3[0]),
        (t0[0] - t2[0], t0[1] - t2[1]),
        (t1[0] - t3[1], t1[1] + t3[0]),
    )


def residues_to_quarters(z):
    t0 = [z[0][k] + z[2][k] for k in range(2)]
    t1 = [z[0][k] - z[2][k] for k in range(2)]
    t2 = [z[1][k] + z[3][k] for k in range(2)]
    t3 = [z[1][k] - z[3][k] for k in range(2)]
    return (
        (t0[0] + t2[0], t0[1] + t2[1]),
        (t1[0] - t3[1], t1[1] + t3[0]),
        (t0[0] - t2[0], t0[1] - t2[1]),
        (t1[0] + t3[1], t1[1] - t3[0]),
    )


def inverse_lines(v, ti_ref):
    z = []
    for m in range(4):
        result = product(triple(*v[m]), ti_ref[m])
        z.append((result[:, :LANES], result[:, LANES:]))
    return residues_to_quarters(z)


def kernel(
    measured, maps, cotangent, mask, pack,
    tf, ti, tft, dz, perm, rep, cz, gc, expand, choose, fold, amask, gmask,
    grad_k, grad_w,
    sampled, masked, own_maps, maps_land, maps_all, lattice, partial_out, partial_land,
    weights, w_in, w_out, state, gathered, slope, centre, taps_saved, hidden, spectrum,
    energy, memory, final, sums, q_plain, q_masked, q_out, q_land, w_send, w_land, w_all,
    pack_send, pack_recv, part_send, part_recv, maps_send, maps_recv,
    near_send, near_recv, far_send, far_recv, q_send, q_recv, ws_send, ws_recv, wa_send, wa_recv,
):
    w = lax.axis_index("segment")
    s = lax.axis_index("coil")

    def send(source, target, send_sem, recv_sem, axis, place):
        pltpu.make_async_remote_copy(
            src_ref=source, dst_ref=target, send_sem=send_sem, recv_sem=recv_sem,
            device_id={axis: place}, device_id_type=MESH,
        ).start()

    def finish(extent, sem):
        pltpu.make_async_copy(extent, extent, sem).wait()

    segment_peers = [lax.rem(w + k, WIDTH) for k in range(1, WIDTH)]
    coil_peers = [lax.rem(s + k, COILS) for k in range(1, COILS)]

    barrier = pltpu.get_barrier_semaphore()
    for place in segment_peers:
        pl.semaphore_signal(barrier, inc=1, device_id={"segment": place}, device_id_type=MESH)
    for place in coil_peers:
        pl.semaphore_signal(barrier, inc=1, device_id={"coil": place}, device_id_type=MESH)
    pl.semaphore_wait(barrier, WIDTH - 1 + COILS - 1)

    weights[w] = pack[...]
    for place in segment_peers:
        send(weights.at[w], weights.at[w], pack_send, pack_recv, "segment", place)

    flags = mask[...].astype(F32)
    sampled[...] = lax.dot_general(
        flags, rep[...], (((0,), (0,)), ((), ())), preferred_element_type=F32
    )
    spots = sampled[...]
    for k in range(2):
        masked[0, k] = measured[k] * spots
        masked[1, k] = cotangent[k]
        masked[2, k] = cotangent[k] * spots

    own_maps[...] = jnp.zeros_like(own_maps)
    lattice[...] = jnp.zeros_like(lattice)
    for k in range(2):
        for a in range(4):
            own_maps[2 * a + k, :, :QUARTER] = exact_nt(
                perm[...], maps[k, a * QUARTER : (a + 1) * QUARTER, :]
            )
    here = pl.multiple_of(w * SLICES, SLICES)
    for k in range(8):
        maps_land[s, k] = own_maps[k, pl.ds(here, SLICES), :]

    hidden[...] = jnp.zeros_like(hidden)
    spectra = []
    for m in range(4):
        for field in range(3):
            rows_re = masked[field, 0, pl.ds(m, QUARTER, stride=4), :]
            rows_im = masked[field, 1, pl.ds(m, QUARTER, stride=4), :]
            from_re = exact_nt(cz[w], rows_re)
            from_im = exact_nt(cz[w], rows_im)
            place = pl.ds(field * SLICES, SLICES)
            hidden[place, :QUARTER] = from_re[:16] - from_im[16:]
            hidden[place, LANES : LANES + QUARTER] = from_im[:16] + from_re[16:]
        spectra.append((hidden[:48, :LANES], hidden[:48, LANES : 2 * LANES]))
    images = inverse_lines(spectra, ti)
    for a in range(4):
        map_re, map_im = maps_land[s, 2 * a], maps_land[s, 2 * a + 1]
        for field in range(3):
            re = images[a][0][field * 16 : (field + 1) * 16]
            im = images[a][1][field * 16 : (field + 1) * 16]
            row = field * 8 + 2 * a
            partial_out[pl.ds(row, SLICES, stride=32), :] = map_re * re + map_im * im
            partial_out[pl.ds(row + 1, SLICES, stride=32), :] = map_re * im - map_im * re
        power = map_re * map_re + map_im * map_im
        partial_out[pl.ds(24 + 2 * a, SLICES, stride=32), :] = power
        partial_out[pl.ds(25 + 2 * a, SLICES, stride=32), :] = power

    for place in coil_peers:
        send(
            partial_out.at[pl.ds(pl.multiple_of(place * 32, 32), 32)],
            partial_land.at[s], part_send, part_recv, "coil", place,
        )
    for place in coil_peers:
        send(maps_land.at[s], maps_land.at[s], maps_send, maps_recv, "coil", place)
    partial_land[s] = partial_out[pl.ds(pl.multiple_of(s * 32, 32), 32), :]

    def prepare(step):
        way = (step >= CASC).astype(jnp.int32)
        cascade = jnp.where(step < CASC, step, STEPS - 1 - step)
        raw = weights[cascade]
        lane = lax.broadcasted_iota(jnp.int32, raw.shape, 1)
        turned = pltpu.roll(raw, 64, 1)
        first = jnp.where(lane < 64, raw, turned)
        second = jnp.where(lane < 64, turned, raw)
        enter = jnp.where(way == 0, first, second)
        leave = jnp.where(way == 0, second, first)

        def columns(values):
            high = values.astype(BF16).astype(F32)
            return jnp.concatenate([high, values - high, jnp.zeros((80, LANES), F32)], axis=0)

        flat = columns(enter).T[:64].astype(BF16)
        wide = product(flat, expand[way]).astype(BF16)
        for a in range(4):
            w_in[a * 64 : (a + 1) * 64, :] = wide[:, a * 256 : (a + 1) * 256]
        tall = product(choose[way], columns(leave).astype(BF16))
        for j in range(3):
            block = tall[j * 64 : (j + 1) * 64]
            block = jnp.concatenate([block, block], axis=1) * amask[...]
            w_out[:, j * 256 : (j + 1) * 256] = block.astype(BF16)

    finish(weights.at[pl.ds(0, WIDTH - 1)], pack_recv)
    prepare(jnp.int32(0))

    def near(step):
        for distance in (1, -1, 2, -2):
            place = lax.rem(w + distance + WIDTH, WIDTH)
            send(
                state.at[step, 2], state.at[step, 2 - distance],
                near_send.at[step], near_recv.at[step], "segment", place,
            )

    finish(partial_land.at[pl.ds(0, COILS - 1)], part_recv)
    total = partial_land[0]
    for k in range(1, COILS):
        total = total + partial_land[k]
    state[0, 2] = total[0:8]
    near(0)
    state[CASC, 2] = total[8:16]
    near(CASC)
    energy[...] = total[24:32]
    final[...] = total[16:24]

    for m in range(4):
        kernel_rows = exact_nt(gc[s], sampled[pl.ds(m, QUARTER, stride=4), :])
        lattice[m, 0, :, :QUARTER] = kernel_rows[:16]
        lattice[m, 1, :, :QUARTER] = kernel_rows[16:]

    memory[...] = jnp.zeros_like(memory)
    sums[...] = jnp.zeros_like(sums)
    q_plain[...] = jnp.zeros_like(q_plain)
    q_masked[...] = jnp.zeros_like(q_masked)

    def normal(step):
        for block in range(4):
            p = []
            for a in range(4):
                res, ims = [], []
                for inner in range(4):
                    other = block * 4 + inner
                    re = gathered[step, other, 2 * a : 2 * a + 1, :]
                    im = gathered[step, other, 2 * a + 1 : 2 * a + 2, :]
                    map_re = maps_all[2 * a, pl.ds(other * 16, 16), :]
                    map_im = maps_all[2 * a + 1, pl.ds(other * 16, 16), :]
                    res.append(map_re * re - map_im * im)
                    ims.append(map_re * im + map_im * re)
                p.append((jnp.concatenate(res, axis=0), jnp.concatenate(ims, axis=0)))
            z = quarters_to_residues(p)
            for m in range(4):
                spectrum[m, pl.ds(block * 64, 64), :] = triple(*z[m])
        v = []
        for m in range(4):
            x = product(spectrum[m], tf[m])
            re = jnp.zeros((16, LANES), F32)
            im = jnp.zeros((16, LANES), F32)
            for other in range(SLICES):
                g_re = lattice[m, 0, other : other + 1, :]
                g_im = lattice[m, 1, other : other + 1, :]
                x_re = x[other * 16 : (other + 1) * 16, :LANES]
                x_im = x[other * 16 : (other + 1) * 16, LANES:]
                re = re + (g_re * x_re - g_im * x_im)
                im = im + (g_re * x_im + g_im * x_re)
            v.append((re, im))
        y = inverse_lines(v, ti)
        rows = []
        mine = pl.ds(pl.multiple_of(s * 16, 16), 16)
        for a in range(4):
            map_re, map_im = maps_all[2 * a, mine, :], maps_all[2 * a + 1, mine, :]
            rows.append(jnp.sum(map_re * y[a][0] + map_im * y[a][1], axis=0, keepdims=True))
            rows.append(jnp.sum(map_re * y[a][1] - map_im * y[a][0], axis=0, keepdims=True))
        return jnp.concatenate(rows, axis=0)

    def cascade_of(step):
        return jnp.where(step < CASC, step, STEPS - 1 - step)

    def step_size(cascade):
        return weights[cascade, 18:19, :]

    def collect(cascade):
        keep = 1.0 - step_size(cascade)
        slot = STEPS - 1 - cascade
        images = gathered[slot].reshape(SLICES * 8, LANES)
        q_plain[...] = q_plain[...] + images
        q_masked[...] = q_masked[...] * keep + images
        q_out[cascade, 0] = q_plain[...]
        q_out[cascade, 1] = q_masked[...]

        @pl.when(w == cascade)
        def _():
            q_land[w] = q_out[cascade]

        @pl.when(w != cascade)
        def _():
            send(
                q_out.at[cascade], q_land.at[w], q_send.at[cascade], q_recv, "segment", cascade
            )

    def turn(step, carry):
        backward = step >= CASC
        cascade = cascade_of(step)
        finish(state.at[step, pl.ds(0, 4)], near_recv.at[step])

        taps = []
        for column in range(5):
            place = w + (column - 2)
            tile = state[step, column]
            tile = jnp.where((place >= 0) & (place < WIDTH), tile, jnp.zeros_like(tile))
            before, after = shifted(tile)
            taps += [before, tile, after]
        taps = jnp.concatenate(taps, axis=0)
        high = taps.astype(BF16).astype(F32)
        low = taps - high
        rest = jnp.zeros((40, LANES), F32)
        columns = []
        for j in range(3):
            span = slice(24 * j, 24 * j + 72)
            columns.append(jnp.concatenate([high[span], low[span], high[span], rest], axis=0))
        operand = jnp.concatenate(columns, axis=1).astype(BF16)
        lane = lax.broadcasted_iota(jnp.int32, (256, 3 * LANES), 1)
        place = w + lane // LANES - 1
        inside = (place >= 0) & (place < WIDTH)

        @pl.when(jnp.logical_not(backward))
        def _():
            before = product(w_in[...], operand)
            gate = 1.0 / (1.0 + jnp.exp(-before))
            after = before * gate
            zero = jnp.zeros_like(before)
            hidden[...] = jnp.where(inside, after, zero)
            slope[cascade] = jnp.where(inside, gate + after * (1.0 - gate), zero)
            centre[cascade] = after[:, LANES : 2 * LANES]
            taps_saved[cascade] = taps[24:96]

        @pl.when(backward)
        def _():
            hidden[...] = product(w_in[...], operand) * slope[cascade]

        @pl.when(step != CASC - 1)
        def _():
            stack = jnp.concatenate([hidden[:, j * LANES : (j + 1) * LANES] for j in range(3)], axis=0)
            stack_high, stack_low = parts(stack)
            first = product(w_out[...], stack_high)
            second = product(w_out[0:32, :], stack_low)
            response = first[0:24] + first[32:56] + second[0:24]
            before, _ = shifted(response[0:8])
            _, after = shifted(response[16:24])
            gathered[step, s] = before + response[8:16] + after

        @pl.when((step < CASC - 2) | backward)
        def _():
            for place in coil_peers:
                send(
                    gathered.at[step, s], gathered.at[step, s],
                    far_send.at[step], far_recv.at[step], "coil", place,
                )

        @pl.when(step == 1)
        def _():
            finish(maps_land.at[pl.ds(0, COILS - 1)], maps_recv)
            for coil in range(COILS):
                for k in range(8):
                    maps_all[k, pl.ds(coil, SLICES, stride=16), :] = maps_land[coil, k]

        older = step - 1
        once = (step >= 1) & (step < CASC - 1)
        again = (step >= CASC + 1) & (step < STEPS - 1)

        @pl.when(once | again)
        def _():
            finish(gathered.at[older, pl.ds(0, COILS - 1)], far_recv.at[older])
            memory[...] = memory[...] * (1.0 - step_size(cascade_of(older))) + normal(older)

        @pl.when((step != CASC - 1) & (step != STEPS - 1))
        def _():
            answer = gathered[step, s]
            state[step + 1, 2] = (
                state[step, 2] - step_size(cascade) * memory[...] + energy[...] * answer
            )
            near(step + 1)

        @pl.when(step < CASC - 1)
        def _():
            sums[step + 1] = sums[step] * (1.0 - step_size(cascade)) + gathered[step, s]
            prepare(step + 1)

        @pl.when(step == CASC - 1)
        def _():
            memory[...] = final[...]
            prepare(step + 1)

        @pl.when(backward)
        def _():
            @pl.when(step < STEPS - 1)
            def _():
                prepare(step + 1)

            pad = jnp.zeros((56, LANES), F32)
            grads = []
            pairs = (
                (hidden[:, LANES : 2 * LANES], taps_saved[cascade]),
                (centre[cascade], taps[24:96]),
            )
            for values, around in pairs:
                left_high, left_low = parts(values)
                right_high, right_low = parts(jnp.concatenate([around, pad], axis=0))
                full = product_nt(
                    jnp.concatenate([left_high, left_low, left_high], axis=1),
                    jnp.concatenate([right_high, right_high, right_low], axis=1),
                ) * gmask[...]
                grads.append(full[0:64] + full[64:128] + full[128:192] + full[192:256])
            grads = jnp.concatenate(grads, axis=0)
            first = exact_nt(fold[0], grads)
            second = exact_nt(fold[1], grads)
            lanes = lax.broadcasted_iota(jnp.int32, (24, LANES), 1)
            rows = lax.broadcasted_iota(jnp.int32, (24, LANES), 0)
            sizes = -jnp.sum(sums[cascade] * memory[...], axis=0, keepdims=True)
            w_send[cascade] = jnp.where(
                rows == 18, sizes, jnp.where(lanes < 64, first, second)
            )

            @pl.when(w == cascade)
            def _():
                w_land[w] = w_send[cascade]

            @pl.when(w != cascade)
            def _():
                send(
                    w_send.at[cascade], w_land.at[w], ws_send.at[cascade], ws_recv,
                    "segment", cascade,
                )

            @pl.when(step == STEPS - 1)
            def _():
                finish(gathered.at[older, pl.ds(0, COILS - 1)], far_recv.at[older])

            @pl.when(step > CASC)
            def _():
                collect(cascade + 1)

        return carry

    lax.fori_loop(0, STEPS, turn, jnp.int32(0))

    finish(gathered.at[STEPS - 1, pl.ds(0, COILS - 1)], far_recv.at[STEPS - 1])
    collect(jnp.int32(0))

    finish(w_land.at[pl.ds(0, WIDTH - 1)], ws_recv)
    total = w_land[0]
    for k in range(1, WIDTH):
        total = total + w_land[k]
    w_all[s] = total
    for place in coil_peers:
        send(w_all.at[s], w_all.at[s], wa_send, wa_recv, "coil", place)

    keep = jnp.ones((1, LANES), F32)
    for cascade in range(CASC):
        factor = 1.0 - step_size(cascade)
        keep = jnp.where(cascade >= w, keep * factor, keep)

    finish(q_land.at[pl.ds(0, WIDTH - 1)], q_recv)
    p = []
    for a in range(4):
        map_re, map_im = own_maps[2 * a], own_maps[2 * a + 1]
        res, ims = [], []
        for image in range(2):
            q = [
                jnp.concatenate(
                    [q_land[k, image, pl.ds(2 * a + part, SLICES, stride=8), :] for k in range(WIDTH)],
                    axis=0,
                )
                for part in range(2)
            ]
            res.append(map_re * q[0] - map_im * q[1])
            ims.append(map_re * q[1] + map_im * q[0])
        p.append((jnp.concatenate(res, axis=0), jnp.concatenate(ims, axis=0)))
    z = quarters_to_residues(p)
    for m in range(4):
        lines = product_nt(tft[m], triple(*z[m]))
        outs = []
        for image in range(2):
            span = slice(image * LANES, (image + 1) * LANES)
            field = product(
                triple(lines[0:QUARTER, span], lines[LANES : LANES + QUARTER, span]), dz[...]
            )
            outs.append((field[:, :LANES], field[:, LANES:]))
        rows = pl.ds(m, QUARTER, stride=4)
        spots = sampled[rows, :]
        for k in range(2):
            seed = cotangent[k, rows, :]
            grad_k[k, rows, :] = jnp.where(spots > 0.5, keep * seed + outs[1][k], seed + outs[0][k])

    finish(w_all.at[pl.ds(0, COILS - 1)], wa_recv)
    total = w_all[0]
    for k in range(1, COILS):
        total = total + w_all[k]
    grad_w[...] = total

    finish(weights.at[pl.ds(0, WIDTH - 1)], pack_send)
    finish(partial_land.at[pl.ds(0, COILS - 1)], part_send)
    finish(maps_land.at[pl.ds(0, COILS - 1)], maps_send)
    finish(w_all.at[pl.ds(0, COILS - 1)], wa_send)

    def drain(step, carry):
        @pl.when((step < CASC - 2) | (step >= CASC))
        def _():
            finish(gathered.at[step, pl.ds(0, COILS - 1)], far_send.at[step])

        finish(state.at[step, pl.ds(0, 4)], near_send.at[step])

        @pl.when((step < CASC) & (step != w))
        def _():
            finish(q_out.at[step % CASC], q_send.at[step % CASC])
            finish(w_send.at[step % CASC], ws_send.at[step % CASC])

        return carry

    lax.fori_loop(0, STEPS, drain, jnp.int32(0))


def shards(measured, maps, mask, first_filters, second_filters, step_sizes, cotangent):
    body = jnp.concatenate([first_filters[0].T, second_filters[0]], axis=1)
    steps = jnp.broadcast_to(step_sizes[0], (6, LANES))
    pack = jnp.concatenate([body, steps], axis=0)
    tables = [jnp.asarray(table) for table in constants()]
    dma = pltpu.SemaphoreType.DMA
    scratch = [
        pltpu.VMEM((LINES, LANES), F32),
        pltpu.VMEM((3, 2, LINES, LANES), F32),
        pltpu.VMEM((8, LANES, LANES), F32),
        pltpu.VMEM((COILS, 8, SLICES, LANES), F32),
        pltpu.VMEM((8, SLICES * COILS, LANES), F32),
        pltpu.VMEM((4, 2, SLICES, LANES), F32),
        pltpu.VMEM((SLICES * 32, LANES), F32),
        pltpu.VMEM((COILS, 32, LANES), F32),
        pltpu.VMEM((CASC, 24, LANES), F32),
        pltpu.VMEM((256, 256), BF16),
        pltpu.VMEM((64, 768), BF16),
        pltpu.VMEM((STEPS, 5, 8, LANES), F32),
        pltpu.VMEM((STEPS, SLICES, 8, LANES), F32),
        pltpu.VMEM((CASC, 256, 3 * LANES), F32),
        pltpu.VMEM((CASC, 256, LANES), F32),
        pltpu.VMEM((CASC, 72, LANES), F32),
        pltpu.VMEM((256, 3 * LANES), F32),
        pltpu.VMEM((4, 256, 768), BF16),
        pltpu.VMEM((8, LANES), F32),
        pltpu.VMEM((8, LANES), F32),
        pltpu.VMEM((8, LANES), F32),
        pltpu.VMEM((CASC, 8, LANES), F32),
        pltpu.VMEM((SLICES * 8, LANES), F32),
        pltpu.VMEM((SLICES * 8, LANES), F32),
        pltpu.VMEM((CASC, 2, SLICES * 8, LANES), F32),
        pltpu.VMEM((WIDTH, 2, SLICES * 8, LANES), F32),
        pltpu.VMEM((CASC, 24, LANES), F32),
        pltpu.VMEM((WIDTH, 24, LANES), F32),
        pltpu.VMEM((COILS, 24, LANES), F32),
        dma, dma, dma, dma, dma, dma,
        dma((STEPS,)), dma((STEPS,)), dma((STEPS,)), dma((STEPS,)),
        dma((CASC,)), dma, dma((CASC,)), dma, dma, dma,
    ]
    whole = pl.BlockSpec(memory_space=pltpu.VMEM)
    operands = [measured[0], maps[0], cotangent[0], mask, pack] + tables
    grad_k, grad_w = pl.pallas_call(
        kernel,
        out_shape=[
            jax.ShapeDtypeStruct((2, LINES, LANES), F32),
            jax.ShapeDtypeStruct((24, LANES), F32),
        ],
        in_specs=[whole] * len(operands),
        out_specs=[whole, whole],
        scratch_shapes=scratch,
        compiler_params=pltpu.CompilerParams(
            collective_id=0, has_side_effects=True, vmem_limit_bytes=48 * 1024 * 1024
        ),
        name="cascades",
    )(*operands)
    first = grad_w[:18, :64].T
    second = grad_w[:18, 64:]
    return grad_k[None, None], first[None], second[None], jnp.sum(grad_w[18]).reshape(1)


def solution(mesh):
    in_specs = (
        P("coil", None, None, None),
        P("coil", None, None, None),
        P(),
        P("segment", None, None),
        P("segment", None, None),
        P("segment"),
        P("coil", None, None, None),
    )
    out_specs = (
        P("segment", "coil", None, None, None),
        P("segment", None, None),
        P("segment", None, None),
        P("segment"),
    )
    return jax.shard_map(shards, mesh=mesh, in_specs=in_specs, out_specs=out_specs, check_vma=False)
```

time: 2210 us -> 157 us (0.07)
  waiting for transfers between devices: 1090 us -> 0 us
  matrix products: 446 us -> 0 us
  blocking collectives: 446 us -> 0 us
  Pallas kernels: 0 us -> 135 us
  local copies, waits for them, and re-layouts: 117 us -> 18.7 us
  starting transfers between devices: 37.8 us -> 0 us
  other arithmetic: 34.2 us -> 0.68 us
  between operations: 25.8 us -> 1.31 us
    reduce_scatter x16 -> x0, waiting for transfers between devices: 959 us -> none  [collect(): lax.psum_scatter(partial_image, 'coil', scatter_dimension=2, tiled=True)]
    dot_general x295 -> x0, matrix products: 446 us -> none  [the longest x124 348 us: multiply_lines(): return jnp.einsum('uh,chx->cux', table, operand, precision=PRECISE)]
    all_gather x15 -> x0, blocking collectives: 384 us -> none  [return_field(): lax.all_gather(refined, 'coil', axis=2, tiled=True)]
    pallas_call x0 -> x1, Pallas kernels: none -> 135 us  [shards(): pl.pallas_call(kernel, out_shape=[jax.ShapeDtypeStruct((2, LINES, LANES),...]
    ppermute x14 -> x0, waiting for transfers between devices: 127 us -> none  [from_behind(): return lax.ppermute(block, axis, route)]
    psum x1 -> x0, blocking collectives: 62.6 us -> none  [shards(): lax.psum((grad_in, grad_out, grad_step), 'coil')]
    ppermute x14 -> x0, starting transfers between devices: 33.6 us -> none  [from_behind(): return lax.ppermute(block, axis, route)]
    reshape x51 -> x0, local copies, waits for them, and re-layouts: 27.2 us -> none  [the longest x16 10.1 us: network(): stacked = jnp.transpose(stacked, (1, 0, 2)).reshape(18, picture.shape[-1])]
  transfers between devices with their start and end apart: 30 -> 0, of which waited for: 30 -> 0; matrix products, arithmetic and copies ran while one was open for 1% -> 0% of each run, Pallas kernels for 0% -> 0%
where the time goes in v1:
time: 157 us; the launch traced here: 156 us
  Pallas kernels  135 us (86%)
  local copies, waits for them, and re-layouts  18.7 us (12%)
    pallas_call x1, Pallas kernels, shards(): pl.pallas_call(kernel, out_shape=[jax.ShapeDtypeStruct((2, LINES, LANES),...  135 us
    unnamed x37, local copies, waits for them, and re-layouts  18.6 us

profile of v1, /device:TPU:1, one launch (start us, length us, event | category | flops | bytes accessed | tf_op | source)
XLA Modules:
  0.0 155.9 jit_solution(13241706164070500771)
XLA Ops:
  0.6 0.7 copy.30
  1.3 0.7 copy.31
  2.7 0.1 select_maximum_fusion.pack
  2.8 0.0 copy-start
  2.8 1.4 copy-done
  4.2 0.0 copy-start.1
  4.2 1.4 copy-done.1
  5.6 0.0 copy-start.2
  5.6 1.0 copy-done.2
  6.6 0.0 copy-start.3
  6.6 1.0 copy-done.3
  7.6 0.0 copy-start.4
  7.6 1.0 copy-done.4
  8.6 0.0 copy-start.5
  8.6 1.0 copy-done.5
  9.6 0.0 copy-start.6
  9.6 1.0 copy-done.6
  10.5 0.9 copy-done.7
  11.5 0.9 copy-done.8
  12.4 0.9 copy-done.9
  13.3 0.9 copy-done.10
  14.2 0.8 copy-done.11
  15.0 0.8 copy-done.12
  15.9 0.7 copy-done.13
  16.6 0.7 copy-done.14
  17.3 0.7 copy-done.15
  18.0 135.2 %cascades.1 = (f32[2,320,128]{2,1,0:T(8,128)S(1)}, f32[24,128]{1,0:T(8,128)S(1)}) custom-call(f32[2,320,128]{2,1,0:T(8,128)S(1)} %bitcast.21, f32[2,320,128]{2,1,0:T(8,128)S(1)} %bitcast.22, f32[2,320,128]{2,1,0:T(8,128)S(1)} %bitcast.23, s32[16,320]{1,0:T(8,128)S(1)} %copy-done.13, f32[24,128]{1,0:T(8,128)S(1)} %select_maximum_fusion.pack, ...), custom_call_target="tpu_custom_call" | custom-call | tf_op jit(solution)/shard_map/cascades/pallas_call | solution.py:669
  153.3 0.1 slice_bitcast_fusion
  153.4 0.6 copy.24
  154.0 0.6 copy.25
  154.6 0.6 slice_reduce_fusion
  155.2 0.7 copy.34
  (9 shorter events, 0.0 us)
Async XLA Ops:
  2.8 1.4 copy-start
  4.2 1.4 copy-start.1
  5.6 1.0 copy-start.2
  6.6 1.0 copy-start.3
  7.6 1.0 copy-start.4
  8.6 1.0 copy-start.5
  9.6 1.0 copy-start.6
  10.5 0.9 copy-start.7
  11.5 0.9 copy-start.8
  12.4 0.9 copy-start.9
  13.3 0.9 copy-start.10
  14.2 0.8 copy-start.11
  15.0 0.8 copy-start.12
  15.9 0.7 copy-start.13
  16.6 0.7 copy-start.14
  17.3 0.7 copy-start.15

commit v2 on v1

v2 whole, which is shorter than its diff:
```python
import functools

import jax
import jax.numpy as jnp
import ml_dtypes
import numpy as np
from jax import lax
from jax.experimental import pallas as pl
from jax.experimental.pallas import tpu as pltpu
from jax.sharding import PartitionSpec as P

F32 = jnp.float32
BF16 = jnp.bfloat16
LINES = 320
QUARTER = 80
LANES = 128
WIDTH = 8
SLICES = 16
COILS = 16
CASC = 8
STEPS = 2 * CASC
HIDDEN = 64
MESH = pl.DeviceIdType.MESH
AROUND = sorted(
    [(dy, dx) for dy in range(4) for dx in range(4) if dy or dx],
    key=lambda d: -(min(d[0], 4 - d[0]) + min(d[1], 4 - d[1])),
)
LONG = 11
ROWS = (0, 1, 3, 2)


def stacked(table):
    high = table.astype(ml_dtypes.bfloat16)
    low = (table - high.astype(np.float64)).astype(ml_dtypes.bfloat16)
    return np.concatenate([high, high, low], axis=-2)


@functools.lru_cache(maxsize=None)
def constants():
    forward = np.zeros((4, 256, 256))
    inverse = np.zeros((4, 256, 256))
    v = np.arange(QUARTER)[:, None]
    b = np.arange(QUARTER)[None, :]
    re, im = slice(0, QUARTER), slice(LANES, LANES + QUARTER)
    for m in range(4):
        angle = 2 * np.pi * (((4 * v + m) * b) % LINES) / LINES
        cosine = np.cos(angle) / np.sqrt(LINES)
        sine = np.sin(angle) / np.sqrt(LINES)
        forward[m, re, re] = cosine.T
        forward[m, re, im] = -sine.T
        forward[m, im, re] = sine.T
        forward[m, im, im] = cosine.T
        inverse[m, re, re] = cosine
        inverse[m, re, im] = sine
        inverse[m, im, re] = -sine
        inverse[m, im, im] = cosine
    tf = stacked(forward)
    ti = stacked(inverse)
    tft = np.ascontiguousarray(np.swapaxes(tf, 1, 2))

    dz = np.zeros((256, 256))
    for w in range(WIDTH):
        for s in range(SLICES):
            for kz in range(SLICES):
                angle = 2 * np.pi * (s * kz % SLICES) / SLICES
                row, lane = w * SLICES + s, kz * WIDTH + w
                dz[row, lane] = np.cos(angle) / 4
                dz[row, LANES + lane] = -np.sin(angle) / 4
                dz[LANES + row, lane] = np.sin(angle) / 4
                dz[LANES + row, LANES + lane] = np.cos(angle) / 4
    dz = stacked(dz)

    rep = np.zeros((SLICES, LANES), np.float32)
    for kz in range(SLICES):
        rep[kz, kz * WIDTH : (kz + 1) * WIDTH] = 1
    outward = np.zeros((16, 48, LANES), np.float32)
    for g in range(WIDTH):
        for x_hi in range(2):
            for q in range(16):
                j = q % 8
                s = 2 * j + (g % 2 if j % 2 == x_hi else 1 - g % 2)
                w = 2 * (g // 2) + q // 8
                outward[2 * g + x_hi, 32 + q, s * WIDTH + w] = 1
                for kz in range(SLICES):
                    angle = 2 * np.pi * (s * kz % SLICES) / SLICES
                    outward[2 * g + x_hi, q, kz * WIDTH + w] = np.cos(angle) / 4
                    outward[2 * g + x_hi, 16 + q, kz * WIDTH + w] = np.sin(angle) / 4
    gc = np.zeros((SLICES, 32, LANES), np.float32)
    for kz in range(SLICES):
        for s in range(SLICES):
            for n in range(SLICES):
                other = 4 * ((s // 4 + ROWS[n // 4]) % 4) + n % 4
                angle = 2 * np.pi * ((s - other) * kz % SLICES) / SLICES
                gc[s, n, kz * WIDTH] = np.cos(angle) / 16
                gc[s, 16 + n, kz * WIDTH] = np.sin(angle) / 16

    expand = np.zeros((2, LANES, 4 * 256), np.float32)
    choose = np.zeros((2, 3 * 64, LANES), np.float32)
    fold = np.zeros((2, 24, LANES), np.float32)
    amask = np.zeros((64, 256), np.float32)
    gmask = np.zeros((256, LANES), np.float32)
    for ch in range(2):
        for dh in range(3):
            for dw in range(3):
                taps = (ch * 9 + dh * 3 + dw, ch * 9 + (2 - dh) * 3 + (2 - dw))
                for way in range(2):
                    for a in range(4):
                        lane = dw * 24 + dh * 8 + a * 2 + ch
                        expand[way, taps[way], a * 256 + lane] = 1
                        expand[way, taps[way], a * 256 + 72 + lane] = 1
                        expand[way, 24 + taps[way], a * 256 + 144 + lane] = 1
                        fold[way, taps[way], lane] = 1
                        for hl in range(2):
                            row = hl * 32 + dh * 8 + a * 2 + ch
                            choose[way, dw * 64 + row, hl * 24 + taps[way]] = 1
                            amask[row, a * 64 : (a + 1) * 64] = 1
                        gmask[a * 64 : (a + 1) * 64, lane] = 1
    bf = ml_dtypes.bfloat16
    wide = np.concatenate([tf.reshape(-1, 256), ti.reshape(-1, 256), dz], axis=0)
    misc = np.concatenate(
        [rep, fold.reshape(48, LANES), gmask, amask[:, :LANES], amask[:, LANES:]], axis=0
    )
    return wide, tft, expand.astype(bf), choose.astype(bf), misc, outward, gc


def product(left, right):
    return jnp.dot(left, right, preferred_element_type=F32)


def product_nt(left, right):
    return lax.dot_general(left, right, (((1,), (1,)), ((), ())), preferred_element_type=F32)


def parts(values):
    high = values.astype(BF16)
    low = (values - high.astype(F32)).astype(BF16)
    return high, low


def three(values):
    first = values.astype(BF16)
    rest = values - first.astype(F32)
    second = rest.astype(BF16)
    third = (rest - second.astype(F32)).astype(BF16)
    return jnp.concatenate([first, second, third], axis=1)


def triple(re, im):
    re_high, re_low = parts(re)
    im_high, im_low = parts(im)
    return jnp.concatenate([re_high, im_high, re_low, im_low, re_high, im_high], axis=1)


def shifted(tile):
    lane = lax.broadcasted_iota(jnp.int32, (8, LANES), 1)
    row = lax.broadcasted_iota(jnp.int32, (8, LANES), 0)
    zero = jnp.zeros_like(tile)
    last = QUARTER - 1
    next_first = pltpu.roll(pltpu.roll(tile, last, 1), 6, 0)
    after = jnp.where(
        lane < last,
        pltpu.roll(tile, LANES - 1, 1),
        jnp.where((lane == last) & (row < 6), next_first, zero),
    )
    previous_last = pltpu.roll(pltpu.roll(tile, LANES - last, 1), 2, 0)
    before = jnp.where(
        (lane >= 1) & (lane < QUARTER),
        pltpu.roll(tile, 1, 1),
        jnp.where((lane == 0) & (row >= 2), previous_last, zero),
    )
    return before, after


def quarters_to_residues(p):
    t0 = [p[0][k] + p[2][k] for k in range(2)]
    t1 = [p[0][k] - p[2][k] for k in range(2)]
    t2 = [p[1][k] + p[3][k] for k in range(2)]
    t3 = [p[1][k] - p[3][k] for k in range(2)]
    return (
        (t0[0] + t2[0], t0[1] + t2[1]),
        (t1[0] + t3[1], t1[1] - t3[0]),
        (t0[0] - t2[0], t0[1] - t2[1]),
        (t1[0] - t3[1], t1[1] + t3[0]),
    )


def residues_to_quarters(z):
    t0 = [z[0][k] + z[2][k] for k in range(2)]
    t1 = [z[0][k] - z[2][k] for k in range(2)]
    t2 = [z[1][k] + z[3][k] for k in range(2)]
    t3 = [z[1][k] - z[3][k] for k in range(2)]
    return (
        (t0[0] + t2[0], t0[1] + t2[1]),
        (t1[0] - t3[1], t1[1] + t3[0]),
        (t0[0] - t2[0], t0[1] - t2[1]),
        (t1[0] + t3[1], t1[1] - t3[0]),
    )


def inverse_lines(v, table):
    z = []
    for m in range(4):
        result = product(triple(*v[m]), table(m))
        z.append((result[:, :LANES], result[:, LANES:]))
    return residues_to_quarters(z)


def kernel(
    measured_hbm, maps_hbm, cotangent_hbm, mask_hbm, first_hbm, second_hbm, size_ref,
    wide_hbm, tft_hbm, expand_hbm, choose_hbm, misc_hbm, outward_hbm, gc_hbm,
    grad_k, grad_w,
    measured, maps, cotangent, mask, first_in, second_in,
    wide, tft, expand, choose, misc, outward, gc, load_sem,
    sampled, masked, turned_maps, maps_out, maps_land, maps_all, lattice, picked, partial_out, partial_land,
    ending_out, ending_land,
    weights, w_in, w_out, state, gathered, slope, centre, taps_saved, hidden, spectrum,
    energy, memory, final, sums, q_plain, q_masked, q_out, q_land, q_open, tail_land, late_land,
    w_send, w_land, w_pair, w_all,
    pack_send, pack_recv, part_send, part_recv, end_send, end_recv, maps_send, maps_recv,
    near_send, near_recv, far_send, far_recv, far_late, q_send, q_recv,
    tail_send, tail_recv, late_send, late_recv, pass_send, pass_recv,
    ws_send, ws_recv, wp_send, wp_recv, wa_send, wa_recv,
):
    g = lax.axis_index("segment")
    k = lax.axis_index("coil")
    z, x_lo = lax.div(g, 2), lax.rem(g, 2)
    pair, core = lax.div(k, 2), lax.rem(k, 2)
    y, x_hi = lax.div(pair, 2), lax.rem(pair, 2)
    w = 2 * z + core
    s = 2 * pair + x_lo
    x = 2 * x_hi + x_lo

    def role(at_w, at_s):
        return {
            "segment": 2 * lax.div(at_w, 2) + lax.rem(at_s, 2),
            "coil": 2 * lax.div(at_s, 2) + lax.rem(at_w, 2),
        }

    def around(displacement):
        dy, dx = displacement
        return role(w, 4 * lax.rem(y + dy, 4) + lax.rem(x + dx, 4))

    def place(at_g, at_k):
        return {"segment": at_g, "coil": at_k}

    receivers = []
    for dy in (2, 1, 3, 0):
        for flip in range(2):
            for at_core in range(2):
                if dy or flip:
                    at_k = 4 * lax.rem(y + dy, 4) + 2 * lax.rem(x_hi + flip, 2) + at_core
                    at_g = g if flip == 0 else 2 * z + 1 - x_lo
                    receivers.append((at_g, at_k, at_core))
    receivers.append((g, 2 * pair + 1 - core, 1 - core))
    segment_peers = [lax.rem(g + n, WIDTH) for n in range(1, WIDTH)]

    def send(source, target, send_sem, recv_sem, device):
        pltpu.make_async_remote_copy(
            src_ref=source, dst_ref=target, send_sem=send_sem, recv_sem=recv_sem,
            device_id=device, device_id_type=MESH,
        ).start()

    def finish(extent, sem):
        pltpu.make_async_copy(extent, extent, sem).wait()

    loads = (
        (maps_hbm, maps), (measured_hbm, measured), (mask_hbm, mask), (misc_hbm, misc),
        (outward_hbm.at[2 * g + x_hi], outward), (wide_hbm, wide),
        (first_hbm, first_in), (second_hbm, second_in), (cotangent_hbm, cotangent),
        (gc_hbm.at[s], gc), (expand_hbm, expand), (choose_hbm, choose), (tft_hbm, tft),
    )
    loads = [
        pltpu.make_async_copy(source, target, load_sem.at[n])
        for n, (source, target) in enumerate(loads)
    ]
    for load in loads[:6]:
        load.start()

    barrier = pltpu.get_barrier_semaphore()

    def greet(device):
        pl.semaphore_signal(barrier, inc=1, device_id=device, device_id_type=MESH)

    for dy, dx in AROUND:
        if dx:
            other = lax.rem(x + dx, 4)

            @pl.when(other != 3 - x)
            def _():
                greet(role(w, 4 * lax.rem(y + dy, 4) + other))

    for turn in (2, 1, 3):
        at_z = lax.rem(z + turn, 4)
        greet(place(2 * at_z + 1 - x_lo, k))
        for at_core in range(2):
            greet(place(2 * at_z + x_lo, 2 * pair + at_core))
    for at_g, at_k, _ in receivers:
        greet(place(at_g, at_k))
    for load in loads[6:]:
        load.start()

    def tf(m):
        return wide[m * 768 : (m + 1) * 768, :]

    def ti(m):
        return wide[3072 + m * 768 : 3072 + (m + 1) * 768, :]

    def dz():
        return wide[6144:6912, :]

    blank = jnp.zeros((LANES - QUARTER, LANES), F32)

    def padded(values):
        return jnp.concatenate([values, blank], axis=0)

    loads[0].wait()
    for part in range(2):
        for a in range(4):
            block = padded(maps[part, a * QUARTER : (a + 1) * QUARTER, :])
            turned_maps[2 * a + part] = block.T
    for at_core in range(2):
        lines = [
            turned_maps[plane, pl.ds(2 * z + at_core, SLICES, stride=WIDTH), :]
            for plane in range(8)
        ]
        maps_out[at_core] = jnp.concatenate(lines, axis=0).T[:QUARTER]
    maps_land[k] = maps_out[core]

    for load in loads[1:5]:
        load.wait()
    sampled[...] = lax.dot_general(
        mask[...].astype(F32), misc[0:16], (((0,), (0,)), ((), ())), preferred_element_type=F32
    )
    spots = sampled[...]
    for part in range(2):
        masked[0, part] = measured[part] * spots
    c_high, c_low = parts(outward[0:32, :])
    c_left = jnp.concatenate([c_high, c_high, c_low], axis=1)

    def to_images(fields):
        spectra = []
        for m in range(4):
            rows = pl.ds(m, QUARTER, stride=4)
            blocks = [padded(masked[field, part, rows, :]) for field in fields for part in range(2)]
            high, low = parts(jnp.concatenate(blocks, axis=0))
            both = product_nt(c_left, jnp.concatenate([high, low, high], axis=1))
            res, ims = [], []
            for n in range(len(fields)):
                from_re = both[:, n * 256 : n * 256 + LANES]
                from_im = both[:, n * 256 + LANES : n * 256 + 256]
                res.append(from_re[:16] - from_im[16:])
                ims.append(from_im[:16] + from_re[16:])
            spectra.append((jnp.concatenate(res, axis=0), jnp.concatenate(ims, axis=0)))
        return inverse_lines(spectra, ti)

    def weigh(images, count, out):
        for a in range(4):
            map_re, map_im = picked[2 * a], picked[2 * a + 1]
            for n in range(count):
                re = images[a][0][n * 16 : (n + 1) * 16]
                im = images[a][1][n * 16 : (n + 1) * 16]
                row = n * 8 + 2 * a
                out[pl.ds(row, 16, stride=16), :] = map_re * re + map_im * im
                out[pl.ds(row + 1, 16, stride=16), :] = map_re * im - map_im * re

    pick = outward[32:48, :].astype(BF16)
    for plane in range(8):
        split = three(turned_maps[plane])
        picked[plane] = (
            product(pick, split[:, :LANES])
            + product(pick, split[:, LANES : 2 * LANES])
            + product(pick, split[:, 2 * LANES :])
        )
    for a in range(4):
        power = picked[2 * a] * picked[2 * a] + picked[2 * a + 1] * picked[2 * a + 1]
        partial_out[pl.ds(8 + 2 * a, 16, stride=16), :] = power
        partial_out[pl.ds(9 + 2 * a, 16, stride=16), :] = power
    loads[5].wait()
    weigh(to_images((0,)), 1, partial_out)

    for load in loads[6:8]:
        load.wait()
    hidden[0:64, 0:LANES] = jnp.zeros((64, LANES), F32)
    for tap in range(18):
        hidden[tap : tap + 1, 0:64] = first_in[tap]
        hidden[32 + tap : 33 + tap, 0:64] = second_in[tap]
    row24 = lax.broadcasted_iota(jnp.int32, (24, LANES), 0)
    weights[g] = jnp.where(
        row24 < 18,
        hidden[0:24, 0:LANES] + pltpu.roll(hidden[32:56, 0:LANES], 64, 1),
        jnp.full((24, LANES), size_ref[0], F32),
    )

    pl.semaphore_wait(barrier, 32)

    def block_of(at_k):
        q = lax.rem(at_k, 2) * 8 + lax.div(at_k, 2)
        return pl.ds(pl.multiple_of(q * 16, 16), 16)

    for at_g, at_k, _ in receivers:
        send(
            partial_out.at[block_of(at_k)], partial_land.at[k], part_send, part_recv,
            place(at_g, at_k),
        )
    partial_land[k] = partial_out[block_of(k), :]
    for at_g in segment_peers:
        send(weights.at[g], weights.at[g], pack_send, pack_recv, place(at_g, k))
    for at_g, at_k, at_core in receivers:
        send(maps_out.at[at_core], maps_land.at[k], maps_send, maps_recv, place(at_g, at_k))

    loads[8].wait()
    for part in range(2):
        masked[1, part] = cotangent[part]
        masked[2, part] = cotangent[part] * sampled[...]
    weigh(to_images((1, 2)), 2, ending_out)
    for at_g, at_k, _ in receivers:
        send(
            ending_out.at[block_of(at_k)], ending_land.at[k], end_send, end_recv,
            place(at_g, at_k),
        )
    ending_land[k] = ending_out[block_of(k), :]

    for load in loads[9:]:
        load.wait()
    g_high, g_low = parts(gc[...])
    g_left = jnp.concatenate([g_high, g_low], axis=1)
    for m in range(4):
        spots_m = padded(sampled[pl.ds(m, QUARTER, stride=4), :]).astype(BF16)
        rows = product_nt(g_left, jnp.concatenate([spots_m, spots_m], axis=1))
        lattice[m, 0] = rows[:16]
        lattice[m, 1] = rows[16:]

    def cascade_of(step):
        return jnp.where(step < CASC, step, STEPS - 1 - step)

    def step_size(cascade):
        return weights[cascade, 18:19, :]

    def prepare(step):
        way = (step >= CASC).astype(jnp.int32)
        raw = weights[cascade_of(step)]
        lane = lax.broadcasted_iota(jnp.int32, raw.shape, 1)
        turned = pltpu.roll(raw, 64, 1)
        first = jnp.where(lane < 64, raw, turned)
        second = jnp.where(lane < 64, turned, raw)
        enter = jnp.where(way == 0, first, second)
        leave = jnp.where(way == 0, second, first)

        def columns(values):
            high = values.astype(BF16).astype(F32)
            return jnp.concatenate([high, values - high, jnp.zeros((80, LANES), F32)], axis=0)

        flat = columns(enter).T[:64].astype(BF16)
        spread = product(flat, expand[way]).astype(BF16)
        for a in range(4):
            w_in[a * 64 : (a + 1) * 64, :] = spread[:, a * 256 : (a + 1) * 256]
        tall = product(choose[way], columns(leave).astype(BF16))
        inside = (
            jnp.where(w > 0, 1.0, 0.0), jnp.float32(1.0), jnp.where(w < WIDTH - 1, 1.0, 0.0)
        )
        for j in range(3):
            block = tall[j * 64 : (j + 1) * 64]
            left = block * misc[320:384] * inside[j]
            right = block * misc[384:448] * inside[j]
            w_out[:, j * 256 : j * 256 + LANES] = left.astype(BF16)
            w_out[:, j * 256 + LANES : (j + 1) * 256] = right.astype(BF16)

    finish(weights.at[pl.ds(0, WIDTH - 1)], pack_recv)
    prepare(jnp.int32(0))

    def near(step):
        for distance in (2, -2, 1, -1):
            send(
                state.at[step, 2], state.at[step, 2 - distance],
                near_send.at[step], near_recv.at[step],
                role(lax.rem(w + distance + WIDTH, WIDTH), s),
            )

    def far(step, displacements):
        for displacement in displacements:
            send(
                gathered.at[step, s], gathered.at[step, s],
                far_send.at[step],
                far_late.at[step] if displacement[0] == 2 else far_recv.at[step],
                around(displacement),
            )

    finish(partial_land.at[pl.ds(0, COILS - 1)], part_recv)
    total = partial_land[0]
    for n in range(1, COILS):
        total = total + partial_land[n]
    state[0, 2] = total[0:8]
    near(0)
    energy[...] = total[8:16]
    memory[...] = jnp.zeros_like(memory)
    sums[...] = jnp.zeros_like(sums)
    q_plain[...] = jnp.zeros_like(q_plain)
    q_masked[...] = jnp.zeros_like(q_masked)

    def normal(step):
        v = [[jnp.zeros((16, LANES), F32)] * 2 for _ in range(4)]
        for blocks, count, sem in (((0, 1, 2), 11, far_recv), ((3,), 4, far_late)):
            finish(gathered.at[step, pl.ds(0, count)], sem.at[step])
            for block in blocks:
                row = lax.rem(y + ROWS[block], 4)
                p = []
                for a in range(4):
                    res, ims = [], []
                    for inner in range(4):
                        other = row * 4 + inner
                        re = gathered[step, other, 2 * a : 2 * a + 1, :]
                        im = gathered[step, other, 2 * a + 1 : 2 * a + 2, :]
                        span = pl.ds(pl.multiple_of(other * 16, 16), 16)
                        map_re = maps_all[2 * a, span, :]
                        map_im = maps_all[2 * a + 1, span, :]
                        res.append(map_re * re - map_im * im)
                        ims.append(map_re * im + map_im * re)
                    p.append((jnp.concatenate(res, axis=0), jnp.concatenate(ims, axis=0)))
                residues = quarters_to_residues(p)
                for m in range(4):
                    spectrum[m, pl.ds(block * 64, 64), :] = triple(*residues[m])
            start, size = blocks[0] * 64, len(blocks) * 64
            for m in range(4):
                lines = product(spectrum[m, pl.ds(start, size), :], tf(m))
                re, im = v[m]
                for n in range(size // 16):
                    other = start // 16 + n
                    g_re = lattice[m, 0, other : other + 1, :]
                    g_im = lattice[m, 1, other : other + 1, :]
                    x_re = lines[n * 16 : (n + 1) * 16, :LANES]
                    x_im = lines[n * 16 : (n + 1) * 16, LANES:]
                    re = re + (g_re * x_re - g_im * x_im)
                    im = im + (g_re * x_im + g_im * x_re)
                v[m] = [re, im]
        back = inverse_lines(v, ti)
        rows = []
        mine = pl.ds(pl.multiple_of(s * 16, 16), 16)
        for a in range(4):
            map_re, map_im = maps_all[2 * a, mine, :], maps_all[2 * a + 1, mine, :]
            rows.append(jnp.sum(map_re * back[a][0] + map_im * back[a][1], axis=0, keepdims=True))
            rows.append(jnp.sum(map_re * back[a][1] - map_im * back[a][0], axis=0, keepdims=True))
        return jnp.concatenate(rows, axis=0)

    def arrived(step):
        finish(gathered.at[step, pl.ds(0, 11)], far_recv.at[step])
        finish(gathered.at[step, pl.ds(0, 4)], far_late.at[step])

    def accumulate(older):
        memory[...] = memory[...] * (1.0 - step_size(cascade_of(older))) + normal(older)

    def surroundings(step):
        finish(state.at[step, pl.ds(0, 4)], near_recv.at[step])
        taps = []
        for column in range(5):
            at_w = w + (column - 2)
            tile = state[step, column]
            if column != 2:
                tile = jnp.where((at_w >= 0) & (at_w < WIDTH), tile, jnp.zeros_like(tile))
            before, after = shifted(tile)
            taps += [before, tile, after]
        return jnp.concatenate(taps, axis=0)

    def enter(taps):
        high = taps.astype(BF16).astype(F32)
        low = taps - high
        rest = jnp.zeros((40, LANES), F32)
        columns = []
        for j in range(3):
            span = slice(24 * j, 24 * j + 72)
            columns.append(jnp.concatenate([high[span], low[span], high[span], rest], axis=0))
        return product(w_in[...], jnp.concatenate(columns, axis=1).astype(BF16))

    def leave(step, values):
        stack = jnp.concatenate([values[:, j * LANES : (j + 1) * LANES] for j in range(3)], axis=0)
        stack_high, stack_low = parts(stack)
        first = product(w_out[...], stack_high)
        second = product(w_out[0:32, :], stack_low)
        response = first[0:24] + first[32:56] + second[0:24]
        before, _ = shifted(response[0:8])
        _, after = shifted(response[16:24])
        gathered[step, s] = before + response[8:16] + after

    def activate(cascade, taps):
        before = enter(taps)
        gate = 1.0 / (1.0 + jnp.exp(-before))
        after = before * gate
        slope[cascade] = gate + after * (1.0 - gate)
        centre[cascade] = after[:, LANES : 2 * LANES]
        taps_saved[cascade] = taps[24:96]
        return after

    def advance(step):
        state[step + 1, 2] = (
            state[step, 2] - step_size(cascade_of(step)) * memory[...]
            + energy[...] * gathered[step, s]
        )
        near(step + 1)

    def forward(step, carry):
        leave(step, activate(step, surroundings(step)))

        @pl.when(step < CASC - 2)
        def _():
            far(step, AROUND[:LONG])

        @pl.when(step == 1)
        def _():
            finish(maps_land.at[pl.ds(0, COILS - 1)], maps_recv)
            for coil in range(COILS):
                block = padded(maps_land[coil]).T
                for plane in range(8):
                    maps_all[plane, pl.ds(coil, SLICES, stride=16), :] = block[
                        plane * SLICES : (plane + 1) * SLICES
                    ]

        @pl.when(step >= 1)
        def _():
            accumulate(step - 1)

        advance(step)

        @pl.when(step < CASC - 2)
        def _():
            far(step, AROUND[LONG:])

        @pl.when(step == 2)
        def _():
            finish(ending_land.at[pl.ds(0, COILS - 1)], end_recv)
            total = ending_land[0]
            for n in range(1, COILS):
                total = total + ending_land[n]
            state[CASC, 2] = total[0:8]
            near(CASC)
            final[...] = total[8:16]

        sums[step + 1] = sums[step] * (1.0 - step_size(step)) + gathered[step, s]
        prepare(step + 1)
        return carry

    lax.fori_loop(0, CASC - 1, forward, jnp.int32(0))
    activate(CASC - 1, surroundings(CASC - 1))
    prepare(jnp.int32(CASC))
    memory[...] = final[...]

    def filter_grads(cascade, taps):
        grads = []
        pairs = (
            (hidden[:, LANES : 2 * LANES], taps_saved[cascade]),
            (centre[cascade], taps),
        )
        for values, near_taps in pairs:
            left_high, left_low = parts(values)
            right = jnp.concatenate([near_taps, jnp.zeros((56, LANES), F32)], axis=0)
            right_high, right_low = parts(right)
            full = product_nt(
                jnp.concatenate([left_high, left_low, left_high], axis=1),
                jnp.concatenate([right_high, right_high, right_low], axis=1),
            ) * misc[64:320]
            grads.append(full[0:64] + full[64:128] + full[128:192] + full[192:256])
        fold = misc[16:64].astype(BF16)
        folded = product_nt(
            jnp.concatenate([fold, fold, fold], axis=1), three(jnp.concatenate(grads, axis=0))
        )
        lanes = lax.broadcasted_iota(jnp.int32, (24, LANES), 1)
        sizes = -jnp.sum(sums[cascade] * memory[...], axis=0, keepdims=True)
        w_send[cascade] = jnp.where(
            row24 == 18, sizes, jnp.where(lanes < 64, folded[0:24], folded[24:48])
        )

        @pl.when(g == cascade)
        def _():
            w_land[g] = w_send[cascade]

        @pl.when(g != cascade)
        def _():
            send(
                w_send.at[cascade], w_land.at[g], ws_send.at[cascade], ws_recv, place(cascade, k)
            )

    def collect(cascade):
        keep = 1.0 - step_size(cascade)
        slot = STEPS - 1 - cascade
        images = gathered[slot].reshape(SLICES * 8, LANES)
        q_plain[...] = q_plain[...] + images
        q_masked[...] = q_masked[...] * keep + images
        target = jnp.where((cascade == 1) & (x_lo == 0), 0, cascade)

        @pl.when(lax.rem(target, 2) == x_lo)
        def _():
            q_out[cascade, 0] = q_plain[...].T[:QUARTER]
            q_out[cascade, 1] = q_masked[...].T[:QUARTER]

            @pl.when(g == target)
            def _():
                q_land[z] = q_out[cascade]

            @pl.when(g != target)
            def _():
                send(q_out.at[cascade], q_land.at[z], q_send, q_recv, place(target, k))

    def backward(step, carry):
        cascade = STEPS - 1 - step
        taps = surroundings(step)
        values = enter(taps) * slope[cascade]
        hidden[...] = values
        leave(step, values)
        taps_saved[CASC] = taps[24:96]
        ending = step == STEPS - 1

        @pl.when(jnp.logical_not(ending))
        def _():
            far(step, AROUND[:LONG])

        @pl.when(ending)
        def _():
            @pl.when(z == 0)
            def _():
                tail_land[0] = gathered[step, s]

            @pl.when(z != 0)
            def _():
                send(
                    gathered.at[step, s], tail_land.at[z], tail_send, tail_recv, place(x_lo, k)
                )

        @pl.when((step > CASC) & (step < STEPS - 1))
        def _():
            accumulate(step - 1)

        @pl.when(step < STEPS - 1)
        def _():
            advance(step)

        @pl.when(jnp.logical_not(ending))
        def _():
            far(step, AROUND[LONG:])
            prepare(step + 1)

        filter_grads(cascade, taps_saved[CASC])

        @pl.when(step == STEPS - 1)
        def _():
            arrived(step - 1)

        @pl.when(step > CASC)
        def _():
            collect(cascade + 1)

        return carry

    lax.fori_loop(CASC, STEPS, backward, jnp.int32(0))

    even = [(dy, x_at) for dy in (2, 1, 3, 0) for x_at in (0, 2)]

    @pl.when(z == 0)
    def _():
        finish(tail_land.at[pl.ds(0, 3)], tail_recv)
        for dy, x_at in even:
            at_s = 4 * lax.rem(y + dy, 4) + x_at

            @pl.when(at_s == s)
            def _():
                late_land[core, s] = tail_land[...]

            @pl.when(at_s != s)
            def _():
                send(
                    tail_land, late_land.at[core, s], late_send, late_recv, role(core, at_s)
                )

    finish(w_land.at[pl.ds(0, WIDTH - 1)], ws_recv)
    total = w_land[0]
    for n in range(1, WIDTH):
        total = total + w_land[n]
    w_pair[core] = total
    send(w_pair.at[core], w_pair.at[core], wp_send, wp_recv, place(g, 2 * pair + 1 - core))

    def spread_out(count, image_of, into):
        p = []
        for a in range(4):
            columns = [
                [
                    turned_maps[2 * a + part, pl.ds(at_w, SLICES, stride=WIDTH), :]
                    for at_w in range(WIDTH)
                ]
                for part in range(2)
            ]
            map_re = jnp.concatenate(columns[0], axis=0)
            map_im = jnp.concatenate(columns[1], axis=0)
            res, ims = [], []
            for image in range(count):
                re = image_of(image, 2 * a)
                im = image_of(image, 2 * a + 1)
                res.append(map_re * re - map_im * im)
                ims.append(map_re * im + map_im * re)
            p.append((jnp.concatenate(res, axis=0), jnp.concatenate(ims, axis=0)))
        residues = quarters_to_residues(p)
        for m in range(4):
            lines = product_nt(tft[m], triple(*residues[m]))
            fields = []
            for image in range(count):
                span = slice(image * LANES, (image + 1) * LANES)
                field = product(
                    triple(lines[0:QUARTER, span], lines[LANES : LANES + QUARTER, span]), dz()
                )
                fields.append((field[:, :LANES], field[:, LANES:]))
            into(pl.ds(m, QUARTER, stride=4), fields)

    keep = jnp.ones((1, LANES), F32)
    for cascade in range(CASC):
        factor = 1.0 - step_size(cascade)
        keep = jnp.where(cascade >= g, keep * factor, keep)
    late_factor = jnp.where(g == 0, 1.0 - step_size(0), jnp.ones((1, LANES), F32))

    finish(w_pair.at[0], wp_recv)
    w_all[pair] = w_pair[0] + w_pair[1]
    for dy in (2, 1, 3, 0):
        for dx in (2, 0):
            if dy or dx:
                send(
                    w_all.at[pair], w_all.at[pair], wa_send, wa_recv, around((dy, dx))
                )

    partner = place(g, 2 * pair + 1 - core)
    finish(q_land.at[pl.ds(0, 3)], q_recv)
    for at_z in range(4):
        for image in range(2):
            q_open[core, at_z, image] = padded(q_land[at_z, image]).T
    send(q_open.at[core], q_open.at[core], pass_send.at[0], pass_recv.at[0], partner)
    finish(q_open.at[0], pass_recv.at[0])

    def early(image, plane):
        return jnp.concatenate(
            [
                q_open[n % 2, n // 2, image, pl.ds(plane, SLICES, stride=8), :]
                for n in range(WIDTH)
            ],
            axis=0,
        )

    def first_part(rows, fields):
        on = sampled[rows, :] > 0.5
        for part in range(2):
            seed = cotangent[part, rows, :]
            grad_k[part, rows, :] = jnp.where(
                on, keep * seed + late_factor * fields[1][part], seed + fields[0][part]
            )

    spread_out(2, early, first_part)

    @pl.when(g == 0)
    def _():
        finish(late_land.at[0, pl.ds(0, SLICES - 1)], late_recv)
        send(late_land.at[core], late_land.at[core], pass_send.at[1], pass_recv.at[1], partner)
        finish(late_land.at[0], pass_recv.at[1])

        def late(image, plane):
            return jnp.concatenate(
                [late_land[n % 2, :, n // 2, plane, :] for n in range(WIDTH)], axis=0
            )

        def second_part(rows, fields):
            for part in range(2):
                grad_k[part, rows, :] = grad_k[part, rows, :] + fields[0][part]

        spread_out(1, late, second_part)

    finish(w_all.at[pl.ds(0, 7)], wa_recv)
    total = w_all[0]
    for n in range(1, 8):
        total = total + w_all[n]
    for tap in range(18):
        grad_w[tap] = total[tap : tap + 1]
    grad_w[18] = jnp.broadcast_to(jnp.sum(total[18:19], axis=1, keepdims=True), (1, LANES))

    finish(weights.at[pl.ds(0, WIDTH - 1)], pack_send)
    finish(partial_land.at[pl.ds(0, COILS - 1)], part_send)
    finish(ending_land.at[pl.ds(0, COILS - 1)], end_send)
    finish(maps_land.at[pl.ds(0, COILS - 1)], maps_send)
    finish(w_pair.at[0], wp_send)
    finish(w_all.at[pl.ds(0, 7)], wa_send)
    finish(q_land.at[pl.ds(0, 3)], q_send)
    finish(q_open.at[0], pass_send.at[0])

    @pl.when(z != 0)
    def _():
        finish(tail_land.at[0], tail_send)

    @pl.when((z == 0) & (x_lo == 1))
    def _():
        finish(late_land.at[0, pl.ds(0, 8)], late_send)

    @pl.when(g == 0)
    def _():
        finish(late_land.at[0, pl.ds(0, 7)], late_send)
        finish(late_land.at[0], pass_send.at[1])

    def drain(step, carry):
        @pl.when((step < CASC - 2) | ((step >= CASC) & (step < STEPS - 1)))
        def _():
            finish(gathered.at[step, pl.ds(0, COILS - 1)], far_send.at[step])

        finish(state.at[step, pl.ds(0, 4)], near_send.at[step])

        @pl.when((step < CASC) & (step != g))
        def _():
            finish(w_send.at[lax.rem(step, CASC)], ws_send.at[lax.rem(step, CASC)])

        return carry

    lax.fori_loop(0, STEPS, drain, jnp.int32(0))


def shards(measured, maps, mask, first_filters, second_filters, step_sizes, cotangent):
    tables = [jnp.asarray(table) for table in constants()]
    dma = pltpu.SemaphoreType.DMA
    field = pltpu.VMEM((2, LINES, LANES), F32)
    scratch = [
        field, field, field,
        pltpu.VMEM((SLICES, LINES), jnp.int32),
        pltpu.VMEM((18, 1, HIDDEN), F32),
        pltpu.VMEM((18, 1, HIDDEN), F32),
    ]
    whole_tables = tables[:5]
    scratch += [pltpu.VMEM(table.shape, table.dtype) for table in whole_tables]
    scratch += [
        pltpu.VMEM((48, LANES), F32),
        pltpu.VMEM((32, LANES), F32),
        dma((13,)),
        pltpu.VMEM((LINES, LANES), F32),
        pltpu.VMEM((3, 2, LINES, LANES), F32),
        pltpu.VMEM((8, LANES, LANES), F32),
        pltpu.VMEM((2, QUARTER, LANES), F32),
        pltpu.VMEM((COILS, QUARTER, LANES), F32),
        pltpu.VMEM((8, SLICES * COILS, LANES), F32),
        pltpu.VMEM((4, 2, SLICES, LANES), F32),
        pltpu.VMEM((8, SLICES, LANES), F32),
        pltpu.VMEM((SLICES * 16, LANES), F32),
        pltpu.VMEM((COILS, 16, LANES), F32),
        pltpu.VMEM((SLICES * 16, LANES), F32),
        pltpu.VMEM((COILS, 16, LANES), F32),
        pltpu.VMEM((CASC, 24, LANES), F32),
        pltpu.VMEM((256, 256), BF16),
        pltpu.VMEM((64, 768), BF16),
        pltpu.VMEM((STEPS, 5, 8, LANES), F32),
        pltpu.VMEM((STEPS, SLICES, 8, LANES), F32),
        pltpu.VMEM((CASC, 256, 3 * LANES), F32),
        pltpu.VMEM((CASC, 256, LANES), F32),
        pltpu.VMEM((CASC + 1, 72, LANES), F32),
        pltpu.VMEM((256, 3 * LANES), F32),
        pltpu.VMEM((4, 256, 768), BF16),
        pltpu.VMEM((8, LANES), F32),
        pltpu.VMEM((8, LANES), F32),
        pltpu.VMEM((8, LANES), F32),
        pltpu.VMEM((CASC, 8, LANES), F32),
        pltpu.VMEM((SLICES * 8, LANES), F32),
        pltpu.VMEM((SLICES * 8, LANES), F32),
        pltpu.VMEM((CASC, 2, QUARTER, LANES), F32),
        pltpu.VMEM((4, 2, QUARTER, LANES), F32),
        pltpu.VMEM((2, 4, 2, SLICES * 8, LANES), F32),
        pltpu.VMEM((4, 8, LANES), F32),
        pltpu.VMEM((2, SLICES, 4, 8, LANES), F32),
        pltpu.VMEM((CASC, 24, LANES), F32),
        pltpu.VMEM((WIDTH, 24, LANES), F32),
        pltpu.VMEM((2, 24, LANES), F32),
        pltpu.VMEM((8, 24, LANES), F32),
        dma, dma, dma, dma, dma, dma, dma, dma,
        dma((STEPS,)), dma((STEPS,)), dma((STEPS,)), dma((STEPS,)), dma((STEPS,)),
        dma, dma, dma, dma, dma, dma, dma((2,)), dma((2,)),
        dma((CASC,)), dma, dma, dma, dma, dma,
    ]
    there = pl.BlockSpec(memory_space=pltpu.HBM)
    whole = pl.BlockSpec(memory_space=pltpu.VMEM)
    first = jnp.transpose(first_filters, (2, 0, 1))
    second = jnp.transpose(second_filters, (1, 0, 2))
    operands = [measured[0], maps[0], cotangent[0], mask, first, second]
    grad_k, grad_w = pl.pallas_call(
        kernel,
        out_shape=[
            jax.ShapeDtypeStruct((2, LINES, LANES), F32),
            jax.ShapeDtypeStruct((19, 1, LANES), F32),
        ],
        in_specs=[there] * 6 + [pl.BlockSpec(memory_space=pltpu.SMEM)] + [there] * len(tables),
        out_specs=[whole, whole],
        scratch_shapes=scratch,
        compiler_params=pltpu.CompilerParams(
            collective_id=0, has_side_effects=True, vmem_limit_bytes=58 * 1024 * 1024
        ),
        name="cascades",
    )(*operands, step_sizes, *tables)
    first = jnp.transpose(grad_w[:18, :, :64], (1, 2, 0))
    second = jnp.transpose(grad_w[:18, :, 64:], (1, 0, 2))
    return grad_k[None, None], first, second, grad_w[18, 0, :1]


def solution(mesh):
    in_specs = (
        P("coil", None, None, None),
        P("coil", None, None, None),
        P(),
        P("segment", None, None),
        P("segment", None, None),
        P("segment"),
        P("coil", None, None, None),
    )
    out_specs = (
        P("segment", "coil", None, None, None),
        P("segment", None, None),
        P("segment", None, None),
        P("segment"),
    )
    return jax.shard_map(shards, mesh=mesh, in_specs=in_specs, out_specs=out_specs, check_vma=False)
```

time: 157 us -> 114 us (0.73)
  Pallas kernels: 135 us -> 108 us
  local copies, waits for them, and re-layouts: 18.7 us -> 4.26 us
    pallas_call x1, Pallas kernels: 135 us -> 108 us  [shards(): pl.pallas_call(kernel, out_shape=[jax.ShapeDtypeStruct((2, LINES, LANES),...]
    unnamed x37 -> x1, local copies, waits for them, and re-layouts: 18.6 us -> 1.72 us
where the time goes in v2:
time: 114 us; the launch traced here: 113 us
  Pallas kernels  108 us (95%)
  local copies, waits for them, and re-layouts  4.26 us (4%)
  between operations  1.29 us (1%)
    pallas_call x1, Pallas kernels, shards(): pl.pallas_call(kernel, out_shape=[jax.ShapeDtypeStruct((2, LINES, LANES),...  108 us

profile of v2, /device:TPU:1, one launch (start us, length us, event | category | flops | bytes accessed | tf_op | source)
XLA Modules:
  0.0 113.3 jit_solution(16371521809605150604)
XLA Ops:
  1.3 107.8 %cascades.1 = (f32[2,320,128]{2,1,0:T(8,128)}, f32[19,1,128]{2,1,0:T(1,128)}) custom-call(f32[2,320,128]{2,1,0:T(8,128)} %bitcast.11, f32[2,320,128]{2,1,0:T(8,128)} %bitcast.12, f32[2,320,128]{2,1,0:T(8,128)} %bitcast.13, s32[16,320]{1,0:T(8,128)} %mask_hbm.1, f32[18,1,64]{2,1,0:T(1,128)} %bitcast.15, f32[18,1,64]{2,1,0:T(1,128)} %bitcast.16, ...), custom_call_target="tpu_custom_call" | custom-call | tf_op jit(solution)/shard_map/cascades/pallas_call | solution.py:977
  109.1 1.5 %slice_bitcast_fusion = (f32[1,18,64]{2,0,1:T(1,128)}, f32[1,64,18]{1,0,2:T(1,128)}) fusion(f32[19,1,128]{2,1,0:T(1,128)} %get-tuple-element.7), kind=kLoop, calls=%fused_computation | loop fusion | bytes 18432 | tf_op jit(solution)/shard_map/transpose | solution.py:992
  110.5 1.1 slice.11
  111.6 1.7 %copy.20 = f32[1,1,2,320,128]{4,3,2,1,0:T(8,128)} copy(f32[1,1,2,320,128]{4,3,2,1,0:T(8,128)} %bitcast.14) | data formatting | bytes 655360

commit v3 on v2

--- a/solution.py
+++ b/solution.py
@@ -273,9 +273,6 @@
         pltpu.make_async_copy(source, target, load_sem.at[n])
         for n, (source, target) in enumerate(loads)
     ]
-    for load in loads[:6]:
-        load.start()
-
     barrier = pltpu.get_barrier_semaphore()
 
     def greet(device):
@@ -296,7 +293,7 @@
             greet(place(2 * at_z + x_lo, 2 * pair + at_core))
     for at_g, at_k, _ in receivers:
         greet(place(at_g, at_k))
-    for load in loads[6:]:
+    for load in loads:
         load.start()
 
     def tf(m):
@@ -468,12 +465,16 @@
     finish(weights.at[pl.ds(0, WIDTH - 1)], pack_recv)
     prepare(jnp.int32(0))
 
+    near_places = [
+        (distance, role(lax.rem(w + distance + WIDTH, WIDTH), s)) for distance in (2, -2, 1, -1)
+    ]
+    far_places = {displacement: around(displacement) for displacement in AROUND}
+
     def near(step):
-        for distance in (2, -2, 1, -1):
+        for distance, device in near_places:
             send(
                 state.at[step, 2], state.at[step, 2 - distance],
-                near_send.at[step], near_recv.at[step],
-                role(lax.rem(w + distance + WIDTH, WIDTH), s),
+                near_send.at[step], near_recv.at[step], device,
             )
 
     def far(step, displacements):
@@ -482,7 +483,7 @@
                 gathered.at[step, s], gathered.at[step, s],
                 far_send.at[step],
                 far_late.at[step] if displacement[0] == 2 else far_recv.at[step],
-                around(displacement),
+                far_places[displacement],
             )
 
     finish(partial_land.at[pl.ds(0, COILS - 1)], part_recv)

time: 114 us -> 114 us (level)
  no operation moved by 1% of the time
where the time goes in v3:
time: 114 us
  Pallas kernels  108 us (95%)
  local copies, waits for them, and re-layouts  4.26 us (4%)
  between operations  1.29 us (1%)
    pallas_call x1, Pallas kernels, shards(): pl.pallas_call(kernel, out_shape=[jax.ShapeDtypeStruct((2, LINES, LANES),...  108 us

profile of v3, /device:TPU:1, one launch (start us, length us, event | category | flops | bytes accessed | tf_op | source)
XLA Modules:
  0.0 113.6 jit_solution(3225884393394050776)
XLA Ops:
  1.3 108.1 %cascades.1 = (f32[2,320,128]{2,1,0:T(8,128)}, f32[19,1,128]{2,1,0:T(1,128)}) custom-call(f32[2,320,128]{2,1,0:T(8,128)} %bitcast.11, f32[2,320,128]{2,1,0:T(8,128)} %bitcast.12, f32[2,320,128]{2,1,0:T(8,128)} %bitcast.13, s32[16,320]{1,0:T(8,128)} %mask_hbm.1, f32[18,1,64]{2,1,0:T(1,128)} %bitcast.15, f32[18,1,64]{2,1,0:T(1,128)} %bitcast.16, ...), custom_call_target="tpu_custom_call" | custom-call | tf_op jit(solution)/shard_map/cascades/pallas_call | solution.py:978
  109.4 1.5 %slice_bitcast_fusion = (f32[1,18,64]{2,0,1:T(1,128)}, f32[1,64,18]{1,0,2:T(1,128)}) fusion(f32[19,1,128]{2,1,0:T(1,128)} %get-tuple-element.7), kind=kLoop, calls=%fused_computation | loop fusion | bytes 18432 | tf_op jit(solution)/shard_map/transpose | solution.py:993
  110.8 1.1 slice.11
  111.9 1.7 %copy.20 = f32[1,1,2,320,128]{4,3,2,1,0:T(8,128)} copy(f32[1,1,2,320,128]{4,3,2,1,0:T(8,128)} %bitcast.14) | data formatting | bytes 655360

commit v4 on v2

--- a/solution.py
+++ b/solution.py
@@ -603,7 +603,30 @@
         def _():
             far(step, AROUND[:LONG])
 
-        @pl.when(step == 1)
+        @pl.when(step >= 1)
+        def _():
+            accumulate(step - 1)
+
+        advance(step)
+
+        @pl.when(step < CASC - 2)
+        def _():
+            far(step, AROUND[LONG:])
+
+        @pl.when(step == 2)
+        def _():
+            finish(ending_land.at[pl.ds(0, COILS - 1)], end_recv)
+            total = ending_land[0]
+            for n in range(1, COILS):
+                total = total + ending_land[n]
+            state[CASC, 2] = total[0:8]
+            near(CASC)
+            final[...] = total[8:16]
+
+        sums[step + 1] = sums[step] * (1.0 - step_size(step)) + gathered[step, s]
+        prepare(step + 1)
+
+        @pl.when(step == 0)
         def _():
             finish(maps_land.at[pl.ds(0, COILS - 1)], maps_recv)
             for coil in range(COILS):
@@ -613,28 +636,6 @@
                         plane * SLICES : (plane + 1) * SLICES
                     ]
 
-        @pl.when(step >= 1)
-        def _():
-            accumulate(step - 1)
-
-        advance(step)
-
-        @pl.when(step < CASC - 2)
-        def _():
-            far(step, AROUND[LONG:])
-
-        @pl.when(step == 2)
-        def _():
-            finish(ending_land.at[pl.ds(0, COILS - 1)], end_recv)
-            total = ending_land[0]
-            for n in range(1, COILS):
-                total = total + ending_land[n]
-            state[CASC, 2] = total[0:8]
-            near(CASC)
-            final[...] = total[8:16]
-
-        sums[step + 1] = sums[step] * (1.0 - step_size(step)) + gathered[step, s]
-        prepare(step + 1)
         return carry
 
     lax.fori_loop(0, CASC - 1, forward, jnp.int32(0))

time: 114 us -> 113 us (level)
  no operation moved by 1% of the time
where the time goes in v4:
time: 113 us
  Pallas kernels  108 us (96%)
  local copies, waits for them, and re-layouts  4.26 us (4%)
  between operations  1.29 us (1%)
    pallas_call x1, Pallas kernels, shards(): pl.pallas_call(kernel, out_shape=[jax.ShapeDtypeStruct((2, LINES, LANES),...  108 us

profile of v4, /device:TPU:1, one launch (start us, length us, event | category | flops | bytes accessed | tf_op | source)
XLA Modules:
  0.0 113.3 jit_solution(17207107087202703466)
XLA Ops:
  1.3 107.7 %cascades.1 = (f32[2,320,128]{2,1,0:T(8,128)}, f32[19,1,128]{2,1,0:T(1,128)}) custom-call(f32[2,320,128]{2,1,0:T(8,128)} %bitcast.11, f32[2,320,128]{2,1,0:T(8,128)} %bitcast.12, f32[2,320,128]{2,1,0:T(8,128)} %bitcast.13, s32[16,320]{1,0:T(8,128)} %mask_hbm.1, f32[18,1,64]{2,1,0:T(1,128)} %bitcast.15, f32[18,1,64]{2,1,0:T(1,128)} %bitcast.16, ...), custom_call_target="tpu_custom_call" | custom-call | tf_op jit(solution)/shard_map/cascades/pallas_call | solution.py:978
  109.0 1.5 %slice_bitcast_fusion = (f32[1,18,64]{2,0,1:T(1,128)}, f32[1,64,18]{1,0,2:T(1,128)}) fusion(f32[19,1,128]{2,1,0:T(1,128)} %get-tuple-element.7), kind=kLoop, calls=%fused_computation | loop fusion | bytes 18432 | tf_op jit(solution)/shard_map/transpose | solution.py:993
  110.5 1.1 slice.11
  111.5 1.7 %copy.20 = f32[1,1,2,320,128]{4,3,2,1,0:T(8,128)} copy(f32[1,1,2,320,128]{4,3,2,1,0:T(8,128)} %bitcast.14) | data formatting | bytes 655360
